TPU v7x, 32 devices: a whole 2x2x4 slice. The times are simulated.
32 devices in a mesh: dp: 8 (over z, x), tensor: 4 (over y, core).
Axes of the slice: x: 2, y: 2, z: 4, core: 2. Of those that a mesh axis runs over, the one named last changes fastest.
Arguments:
- inputs: float32 [16384, 1600], P(('dp', 'tensor')), may hold values from -6 to 6
- teacher: float32 [16384, 1600], P(('dp', 'tensor')), may hold values from -6 to 6
- segment_ids: int32 [16384], P('dp'), may hold values from 0 to 23, never falling along the last dimension, each value on 1 to 1536 neighbouring positions
- valid: int32 [16384], P(('dp', 'tensor')), may hold values from 0 to 1, as said below
- norm_in_gain: bfloat16 [1600], P('dp'), may hold values from 0.5 to 1.5
- w_query: bfloat16 [1600, 1600], P('dp'), may hold values from -0.15625 to 0.15625
- w_key: bfloat16 [1600, 320], P('dp'), may hold values from -0.15625 to 0.15625
- w_value: bfloat16 [1600, 320], P('dp'), may hold values from -0.15625 to 0.15625
- w_attn_out: bfloat16 [1600, 1600], P(None, 'dp'), may hold values from -0.15625 to 0.15625
- w_mamba_in: bfloat16 [1600, 2, 3200], P('dp', None, 'tensor'), may hold values from -0.15625 to 0.15625
- conv_weight: bfloat16 [4, 3200], P(None, 'dp'), may hold values from -3 to 3
- conv_bias: bfloat16 [3200], P('dp'), may hold values from -1 to 1
- x_proj: bfloat16 [3200, 132], P('dp'), may hold values from -0.21875 to 0.21875
- dt_proj: bfloat16 [100, 3200], P(None, 'dp'), may hold values from -0.625 to 0.625
- dt_bias: bfloat16 [3200], P('dp'), may hold values from -4 to -0.5
- a_log: bfloat16 [3200], P('dp'), may hold values from -5 to -0.5
- d_skip: bfloat16 [3200], P('dp'), may hold values from 0.5 to 1.5
- w_mamba_out: bfloat16 [3200, 1600], P('tensor', 'dp'), may hold values from -0.109375 to 0.109375
- attn_norm_gain: bfloat16 [1600], P('dp'), may hold values from 0.5 to 1.5
- ssm_norm_gain: bfloat16 [1600], P('dp'), may hold values from 0.5 to 1.5
- norm_mid_gain: bfloat16 [1600], P('dp'), may hold values from 0.5 to 1.5
- w_gate: bfloat16 [1600, 5504], P('dp', 'tensor'), may hold values from -0.15625 to 0.15625
- w_up: bfloat16 [1600, 5504], P('dp', 'tensor'), may hold values from -0.15625 to 0.15625
- w_down: bfloat16 [5504, 1600], P('tensor', 'dp'), may hold values from -0.078125 to 0.078125
Outputs:
- out: float32 [16384, 1600], P(('dp', 'tensor'))
- grad_inputs: float32 [16384, 1600], P(('dp', 'tensor'))
- grad_norm_in_gain: float32 [1600], P('dp')
- grad_w_query: float32 [1600, 1600], P('dp')
- grad_w_key: float32 [1600, 320], P('dp')
- grad_w_value: float32 [1600, 320], P('dp')
- grad_w_attn_out: float32 [1600, 1600], P(None, 'dp')
- grad_w_mamba_in: float32 [1600, 2, 3200], P('dp', None, 'tensor')
- grad_conv_weight: float32 [4, 3200], P(None, 'dp')
- grad_conv_bias: float32 [3200], P('dp')
- grad_x_proj: float32 [3200, 132], P('dp')
- grad_dt_proj: float32 [100, 3200], P(None, 'dp')
- grad_dt_bias: float32 [3200], P('dp')
- grad_a_log: float32 [3200], P('dp')
- grad_d_skip: float32 [3200], P('dp')
- grad_w_mamba_out: float32 [3200, 1600], P('tensor', 'dp')
- grad_attn_norm_gain: float32 [1600], P('dp')
- grad_ssm_norm_gain: float32 [1600], P('dp')
- grad_norm_mid_gain: float32 [1600], P('dp')
- grad_w_gate: float32 [1600, 5504], P('dp', 'tensor')
- grad_w_up: float32 [1600, 5504], P('dp', 'tensor')
- grad_w_down: float32 [5504, 1600], P('tensor', 'dp')
Inputs may be any that keep to these rules, and one draw needn't show every extreme that they name: Every 16th token has valid = 1.
All inputs are finite; a program needn't handle non-finite values.
Results may differ from a plain program's by a relative error of at most 0.02.
The roundings to bfloat16 on the way count: a program that leaves them out, or rounds other values in their place, can miss the bound.
Values may be sent and summed in bfloat16 or wider, within the bound.
A program may use at most 448 MiB of HBM per device.

v0:
```python
import jax
import jax.numpy as jnp
from jax import lax
from jax.sharding import PartitionSpec as P

HEADS = 25
KV = 5
HEAD = 64
STATE = 16
RANK = 100
CONV = 4
WINDOW = 1024
BLOCK = 512
STRETCH = 64
LEN = 2048


EPSILON = 1e-06
MASKED = -1e30
HIGHEST = lax.Precision.HIGHEST


def normalize(values, gain):
    return values * lax.rsqrt(jnp.mean(values * values, axis=-1, keepdims=True) + EPSILON) * gain


def join_rows(resid, attn_sum, ssm_sum, gain_attn, gain_ssm):
    return resid + 0.5 * (normalize(attn_sum, gain_attn) + normalize(ssm_sum, gain_ssm))


def dot_plain(left, right):
    return jnp.dot(left, right, preferred_element_type=jnp.float32)


def dot_last(left, right):
    return lax.dot_general(
        left, right, (((1,), (1,)), ((), ())), preferred_element_type=jnp.float32
    )


def dot_first(left, right):
    return lax.dot_general(
        left, right, (((0,), (0,)), ((), ())), preferred_element_type=jnp.float32
    )


def pick_groups(weight, first_slot, second_slot, group_width, axis):
    return jnp.concatenate(
        [
            lax.dynamic_slice_in_dim(weight, first_slot * group_width, group_width, axis),
            lax.dynamic_slice_in_dim(weight, second_slot * group_width, group_width, axis),
        ],
        axis=axis,
    )


def place_groups(piece, first_slot, second_slot, group_width, full_width, axis):
    new_shape = list(piece.shape)
    new_shape[axis] = full_width
    blank = jnp.zeros(tuple(new_shape), jnp.float32)
    first_part = lax.slice_in_dim(piece, 0, group_width, axis=axis)
    second_part = lax.slice_in_dim(piece, group_width, 2 * group_width, axis=axis)
    return lax.dynamic_update_slice_in_dim(
        blank, first_part, first_slot * group_width, axis
    ) + lax.dynamic_update_slice_in_dim(blank, second_part, second_slot * group_width, axis)


def place_block(piece, start, full_width, axis):
    new_shape = list(piece.shape)
    new_shape[axis] = full_width
    return lax.dynamic_update_slice_in_dim(
        jnp.zeros(tuple(new_shape), jnp.float32), piece, start, axis
    )


def front_pad(values, fill):
    new_shape = (WINDOW,) + values.shape[1:]
    return jnp.concatenate([jnp.full(new_shape, fill, values.dtype), values], axis=0)


def block_mask(block_start, query_seg, key_seg):
    query_pos = block_start + jnp.arange(BLOCK, dtype=jnp.int32)
    key_pos = block_start - WINDOW + jnp.arange(WINDOW + BLOCK, dtype=jnp.int32)
    offset = query_pos[:, None] - key_pos[None, :]
    return (offset >= 0) & (offset < WINDOW) & (query_seg[:, None] == key_seg[None, :])


def attend_forward(pieces):
    queries, keys, values, segs = pieces
    key_pad = front_pad(keys, 0)
    value_pad = front_pad(values, 0)
    seg_pad = front_pad(segs, -1)

    def one_block(block_index):
        block_start = block_index * BLOCK
        query_blk = lax.dynamic_slice_in_dim(queries, block_start, BLOCK, 0)
        key_blk = lax.dynamic_slice_in_dim(key_pad, block_start, WINDOW + BLOCK, 0)
        value_blk = lax.dynamic_slice_in_dim(value_pad, block_start, WINDOW + BLOCK, 0)
        allowed = block_mask(
            block_start,
            lax.dynamic_slice_in_dim(segs, block_start, BLOCK, 0),
            lax.dynamic_slice_in_dim(seg_pad, block_start, WINDOW + BLOCK, 0),
        )
        scores = (
            jnp.einsum("qgjd,kgd->gjqk", query_blk, key_blk, preferred_element_type=jnp.float32)
            * 0.125
        )
        masked = jnp.where(allowed, scores, MASKED)
        row_max = jnp.max(masked, axis=-1, keepdims=True)
        expo = jnp.exp(masked - row_max)
        row_total = jnp.sum(expo, axis=-1, keepdims=True)
        weights = (expo / row_total).astype(jnp.bfloat16)
        result = jnp.einsum(
            "gjqk,kgd->qgjd", weights, value_blk, preferred_element_type=jnp.float32
        )
        return (result.astype(jnp.bfloat16), row_max + jnp.log(row_total))

    return lax.map(one_block, jnp.arange(queries.shape[0] // BLOCK, dtype=jnp.int32))


def attend_backward(pieces):
    queries, keys, values, grad_att, log_totals, segs = pieces
    key_pad = front_pad(keys, 0)
    value_pad = front_pad(values, 0)
    seg_pad = front_pad(segs, -1)
    span_rows = WINDOW + BLOCK

    def one_block(accums, block_index):
        key_acc, value_acc = accums
        block_start = block_index * BLOCK
        query_blk = lax.dynamic_slice_in_dim(queries, block_start, BLOCK, 0)
        grad_blk = lax.dynamic_slice_in_dim(grad_att, block_start, BLOCK, 0)
        key_blk = lax.dynamic_slice_in_dim(key_pad, block_start, span_rows, 0)
        value_blk = lax.dynamic_slice_in_dim(value_pad, block_start, span_rows, 0)
        allowed = block_mask(
            block_start,
            lax.dynamic_slice_in_dim(segs, block_start, BLOCK, 0),
            lax.dynamic_slice_in_dim(seg_pad, block_start, span_rows, 0),
        )
        scores = (
            jnp.einsum("qgjd,kgd->gjqk", query_blk, key_blk, preferred_element_type=jnp.float32)
            * 0.125
        )
        prob_rows = jnp.where(allowed, jnp.exp(scores - log_totals[block_index]), 0.0)
        weights = prob_rows.astype(jnp.bfloat16)
        grad_prob = jnp.einsum(
            "qgjd,kgd->gjqk", grad_blk, value_blk, preferred_element_type=jnp.float32
        )
        delta_rows = jnp.sum(grad_prob * prob_rows, axis=-1, keepdims=True)
        grad_score = (prob_rows * (grad_prob - delta_rows)).astype(jnp.bfloat16)
        grad_query = (
            jnp.einsum("gjqk,kgd->qgjd", grad_score, key_blk, preferred_element_type=jnp.float32)
            * 0.125
        )
        grad_key = (
            jnp.einsum("gjqk,qgjd->kgd", grad_score, query_blk, preferred_element_type=jnp.float32)
            * 0.125
        )
        grad_value = jnp.einsum(
            "gjqk,qgjd->kgd", weights, grad_blk, preferred_element_type=jnp.float32
        )
        key_acc = lax.dynamic_update_slice_in_dim(
            key_acc,
            lax.dynamic_slice_in_dim(key_acc, block_start, span_rows, 0) + grad_key,
            block_start,
            0,
        )
        value_acc = lax.dynamic_update_slice_in_dim(
            value_acc,
            lax.dynamic_slice_in_dim(value_acc, block_start, span_rows, 0) + grad_value,
            block_start,
            0,
        )
        return ((key_acc, value_acc), grad_query)

    zeros_pad = jnp.zeros(key_pad.shape, jnp.float32)
    (key_acc, value_acc), grad_queries = lax.scan(
        one_block, (zeros_pad, zeros_pad), jnp.arange(queries.shape[0] // BLOCK, dtype=jnp.int32)
    )
    return (grad_queries.reshape(queries.shape), key_acc[WINDOW:], value_acc[WINDOW:])


def conv_rows(x_in, conv_w, conv_b, segs_grid):
    seq_count, seq_len = segs_grid.shape
    width = x_in.shape[1]
    grid = x_in.reshape(seq_count, seq_len, width)
    pad_x = jnp.concatenate([jnp.zeros((seq_count, CONV - 1, width), jnp.float32), grid], axis=1)
    pad_seg = jnp.concatenate([jnp.full((seq_count, CONV - 1), -1, jnp.int32), segs_grid], axis=1)
    total = jnp.zeros((seq_count, seq_len, width), jnp.float32) + conv_b
    for tap in range(CONV):
        same = (pad_seg[:, tap : tap + seq_len] == segs_grid).astype(jnp.float32)
        total = total + conv_w[tap] * pad_x[:, tap : tap + seq_len] * same[:, :, None]
    return jax.nn.silu(total).reshape(seq_count * seq_len, width)


def stretch_step(carry_state, piece, decay_rate):
    carried, seg_before = carry_state
    inner_rows, step_rows, input_map, output_map, piece_segs = piece
    piece_len = piece_segs.shape[0]
    positions = jnp.arange(piece_len, dtype=jnp.int32)
    lower_tri = positions[:, None] >= positions[None, :]
    log_decay = -step_rows * decay_rate
    cumulated = jnp.dot(lower_tri.astype(jnp.float32), log_decay, precision=HIGHEST)
    allowed = lower_tri & (piece_segs[:, None] == piece_segs[None, :])
    gap_values = jnp.where(allowed[:, :, None], cumulated[:, None, :] - cumulated[None, :, :], 0.0)
    transfer = jnp.where(allowed[:, :, None], jnp.exp(gap_values), 0.0)
    gram_matrix = jnp.dot(output_map, input_map.T, precision=HIGHEST)
    drive_term = step_rows * inner_rows
    within = jnp.einsum("tsc,ts,sc->tc", transfer, gram_matrix, drive_term, precision=HIGHEST)
    linked = (piece_segs == seg_before).astype(jnp.float32)
    from_state = (
        jnp.exp(cumulated) * jnp.dot(output_map, carried, precision=HIGHEST) * linked[:, None]
    )
    last_seg = piece_segs[piece_len - 1]
    tail_mask = (piece_segs == last_seg).astype(jnp.float32)
    end_decay = cumulated[piece_len - 1]
    pushed = jnp.exp(end_decay[None, :] - cumulated) * tail_mask[:, None] * drive_term
    keep_state = jnp.where(last_seg == seg_before, 1.0, 0.0).astype(jnp.float32)
    fresh_state = jnp.exp(end_decay)[None, :] * carried * keep_state + jnp.dot(
        input_map.T, pushed, precision=HIGHEST
    )
    return ((fresh_state, last_seg), within + from_state)


def scan_sequence(pieces, decay_rate, skip):
    inner_part, gate_part, step_size, maps, segs = pieces
    count = segs.shape[0] // STRETCH
    width = inner_part.shape[1]
    parts = (
        inner_part.reshape(count, STRETCH, width),
        step_size.reshape(count, STRETCH, width),
        maps[:, :STATE].reshape(count, STRETCH, STATE),
        maps[:, STATE:].reshape(count, STRETCH, STATE),
        segs.reshape(count, STRETCH),
    )
    initial = (jnp.zeros((STATE, width), jnp.float32), jnp.array(-1, jnp.int32))
    stepper = jax.checkpoint(stretch_step)
    _, outputs = lax.scan(
        lambda carry_state, piece: stepper(carry_state, piece, decay_rate), initial, parts
    )
    result = outputs.reshape(segs.shape[0], width) + skip * inner_part
    return result * jax.nn.silu(gate_part)


def mamba_rows(x_act, z_gate, x_dbl, dt_weight, vectors, segs_grid):
    seq_count, seq_len = segs_grid.shape
    width = x_act.shape[1]
    step_size = jax.nn.softplus(jnp.dot(x_dbl[:, :RANK], dt_weight, precision=HIGHEST) + vectors[0])
    decay_rate = jnp.exp(vectors[1])
    maps = x_dbl[:, RANK:]

    def one_sequence(pieces):
        return scan_sequence(pieces, decay_rate, vectors[2])

    outputs = lax.map(
        one_sequence,
        (
            x_act.reshape(seq_count, seq_len, width),
            z_gate.reshape(seq_count, seq_len, width),
            step_size.reshape(seq_count, seq_len, width),
            maps.reshape(seq_count, seq_len, 2 * STATE),
            segs_grid,
        ),
    )
    return outputs.reshape(seq_count * seq_len, width)


def per_device(
    inputs,
    teacher,
    segment_ids,
    valid,
    norm_in_gain,
    w_query,
    w_key,
    w_value,
    w_attn_out,
    w_mamba_in,
    conv_weight,
    conv_bias,
    x_proj,
    dt_proj,
    dt_bias,
    a_log,
    d_skip,
    w_mamba_out,
    attn_norm_gain,
    ssm_norm_gain,
    norm_mid_gain,
    w_gate,
    w_up,
    w_down,
):
    rank_index = lax.axis_index("tensor")
    first_slot = jnp.where(rank_index == 0, 0, rank_index + 1)
    second_slot = jnp.where(rank_index == 0, 1, rank_index + 1)
    second_keep = jnp.where(rank_index == 0, 1.0, 0.0).astype(jnp.bfloat16)
    group_width = HEADS // KV * HEAD
    query_width = 2 * group_width
    inner_width = w_mamba_out.shape[0]
    inner_start = rank_index * inner_width
    inner_all = inner_width * lax.axis_size("tensor")
    qkv_local = jnp.concatenate(
        [
            pick_groups(w_query, first_slot, second_slot, group_width, 1),
            pick_groups(w_key, first_slot, second_slot, HEAD, 1),
            pick_groups(w_value, first_slot, second_slot, HEAD, 1),
        ],
        axis=1,
    )
    out_local = pick_groups(w_attn_out, first_slot, second_slot, group_width, 0)
    gains_local = jnp.stack([norm_in_gain, attn_norm_gain, ssm_norm_gain])
    vectors_local = jnp.concatenate(
        [jnp.stack([dt_bias, a_log, d_skip, conv_bias]), conv_weight], axis=0
    )
    (
        qkv_all,
        out_all,
        mamba_in_all,
        mamba_out_all,
        gains_all,
        vectors_all,
        xproj_all,
        dtproj_all,
        gate_all,
        up_all,
        down_all,
        mid_gain_all,
    ) = (
        lax.all_gather(qkv_local, "dp", axis=0, tiled=True),
        lax.all_gather(out_local, "dp", axis=1, tiled=True),
        lax.all_gather(w_mamba_in, "dp", axis=0, tiled=True),
        lax.all_gather(w_mamba_out, "dp", axis=1, tiled=True),
        lax.all_gather(gains_local, "dp", axis=1, tiled=True),
        lax.all_gather(vectors_local, "dp", axis=1, tiled=True),
        lax.all_gather(x_proj, "dp", axis=0, tiled=True),
        lax.all_gather(dt_proj, "dp", axis=1, tiled=True),
        lax.all_gather(w_gate, "dp", axis=0, tiled=True),
        lax.all_gather(w_up, "dp", axis=0, tiled=True),
        lax.all_gather(w_down, "dp", axis=1, tiled=True),
        lax.all_gather(norm_mid_gain, "dp", axis=0, tiled=True),
    )
    valid_total = lax.psum(jnp.sum(valid).astype(jnp.float32), ("dp", "tensor"))
    gain_in = gains_all[0].astype(jnp.float32)
    gain_attn = gains_all[1].astype(jnp.float32)
    gain_ssm = gains_all[2].astype(jnp.float32)
    normed_in, pull_in = jax.vjp(normalize, inputs, gain_in)
    whole_in = lax.all_gather(normed_in.astype(jnp.bfloat16), "tensor", axis=0, tiled=True)
    group_rows = whole_in.shape[0]
    seq_count = group_rows // LEN
    segs_grid = segment_ids.reshape(seq_count, LEN)
    qkv_rows = dot_plain(whole_in, qkv_all).astype(jnp.bfloat16)
    queries = qkv_rows[:, :query_width].reshape(seq_count, LEN, 2, HEADS // KV, HEAD)
    keys_all = qkv_rows[:, query_width : query_width + 2 * HEAD].reshape(seq_count, LEN, 2, HEAD)
    values_all = qkv_rows[:, query_width + 2 * HEAD :].reshape(seq_count, LEN, 2, HEAD)
    attended, log_totals = lax.map(attend_forward, (queries, keys_all, values_all, segs_grid))
    slot_scale = jnp.stack([jnp.ones((), jnp.bfloat16), second_keep]).reshape(1, 2, 1, 1)
    attended = (attended.reshape(group_rows, 2, HEADS // KV, HEAD) * slot_scale).reshape(
        group_rows, query_width
    )
    attn_part = dot_plain(attended, out_all)
    mamba_in_flat = mamba_in_all.reshape(mamba_in_all.shape[0], 2 * inner_width)
    vector_rows = lax.dynamic_slice_in_dim(vectors_all, inner_start, inner_width, 1).astype(
        jnp.float32
    )
    xproj_rows = lax.dynamic_slice_in_dim(xproj_all, inner_start, inner_width, 0)
    dtproj_cols = lax.dynamic_slice_in_dim(dtproj_all, inner_start, inner_width, 1).astype(
        jnp.float32
    )
    mixing = dot_plain(whole_in, mamba_in_flat).reshape(group_rows, 2, inner_width)
    x_pre, pull_conv = jax.vjp(
        lambda x_part, taps, shift: conv_rows(x_part, taps, shift, segs_grid),
        mixing[:, 0],
        vector_rows[4:],
        vector_rows[3],
    )
    x_act = x_pre.astype(jnp.bfloat16)
    x_dbl = lax.psum(dot_plain(x_act, xproj_rows), "tensor").astype(jnp.bfloat16)
    ssm_pre, pull_ssm = jax.vjp(
        lambda act_in, gate_in, dbl_in, proj_in, vec_in: mamba_rows(
            act_in, gate_in, dbl_in, proj_in, vec_in, segs_grid
        ),
        x_act.astype(jnp.float32),
        mixing[:, 1],
        x_dbl.astype(jnp.float32),
        dtproj_cols,
        vector_rows[:3],
    )
    ssm_rows = ssm_pre.astype(jnp.bfloat16)
    ssm_part = dot_plain(ssm_rows, mamba_out_all)
    attn_sum, ssm_sum = (
        lax.psum_scatter(attn_part, "tensor", scatter_dimension=0, tiled=True),
        lax.psum_scatter(ssm_part, "tensor", scatter_dimension=0, tiled=True),
    )
    mixed, pull_join = jax.vjp(join_rows, inputs, attn_sum, ssm_sum, gain_attn, gain_ssm)
    gain_mid = mid_gain_all.astype(jnp.float32)
    normed_mid, pull_mid = jax.vjp(normalize, mixed, gain_mid)
    whole_mid = lax.all_gather(normed_mid.astype(jnp.bfloat16), "tensor", axis=0, tiled=True)
    gate_rows = dot_plain(whole_mid, gate_all)
    up_rows = dot_plain(whole_mid, up_all)
    sigmoid_gate = jax.nn.sigmoid(gate_rows)
    hidden = (gate_rows * sigmoid_gate * up_rows).astype(jnp.bfloat16)
    ffn_rows = lax.psum_scatter(
        dot_plain(hidden, down_all), "tensor", scatter_dimension=0, tiled=True
    )
    result = mixed + ffn_rows
    all_rows = inputs.shape[0] * lax.axis_size("dp") * lax.axis_size("tensor")
    grad_out = all_rows / valid_total * valid.astype(jnp.float32)[:, None] * (result - teacher)
    grad_ffn = lax.all_gather(grad_out.astype(jnp.bfloat16), "tensor", axis=0, tiled=True)
    grad_hidden = dot_last(grad_ffn, down_all)
    grad_gate = (
        grad_hidden * up_rows * sigmoid_gate * (1.0 + gate_rows * (1.0 - sigmoid_gate))
    ).astype(jnp.bfloat16)
    grad_up = (grad_hidden * gate_rows * sigmoid_gate).astype(jnp.bfloat16)
    grad_down_w = dot_first(hidden, grad_ffn)
    grad_gate_w = dot_first(whole_mid, grad_gate)
    grad_up_w = dot_first(whole_mid, grad_up)
    grad_mid_rows = lax.psum_scatter(
        dot_last(grad_gate, gate_all) + dot_last(grad_up, up_all),
        "tensor",
        scatter_dimension=0,
        tiled=True,
    )
    grad_mixed_norm, grad_gain_mid = pull_mid(grad_mid_rows)
    grad_mixed = grad_out + grad_mixed_norm
    grad_resid, grad_attn_sum, grad_ssm_sum, grad_gain_attn, grad_gain_ssm = pull_join(grad_mixed)
    grad_attn_whole, grad_ssm_whole = (
        lax.all_gather(grad_attn_sum.astype(jnp.bfloat16), "tensor", axis=0, tiled=True),
        lax.all_gather(grad_ssm_sum.astype(jnp.bfloat16), "tensor", axis=0, tiled=True),
    )
    grad_out_w = dot_first(attended, grad_attn_whole)
    grad_attended = (
        dot_last(grad_attn_whole, out_all).reshape(group_rows, 2, HEADS // KV, HEAD) * slot_scale
    ).astype(jnp.bfloat16)
    grad_queries, grad_keys, grad_values = lax.map(
        attend_backward,
        (
            queries,
            keys_all,
            values_all,
            grad_attended.reshape(seq_count, LEN, 2, HEADS // KV, HEAD),
            log_totals,
            segs_grid,
        ),
    )
    grad_qkv = jnp.concatenate(
        [
            grad_queries.reshape(group_rows, query_width),
            grad_keys.reshape(group_rows, 2 * HEAD),
            grad_values.reshape(group_rows, 2 * HEAD),
        ],
        axis=1,
    ).astype(jnp.bfloat16)
    grad_qkv_w = dot_first(whole_in, grad_qkv)
    grad_ssm_rows = dot_last(grad_ssm_whole, mamba_out_all)
    grad_mamba_out_w = dot_first(ssm_rows, grad_ssm_whole)
    grad_act_scan, grad_gate_part, grad_dbl_part, grad_dtproj, grad_vectors = pull_ssm(
        grad_ssm_rows
    )
    grad_dbl = lax.psum(grad_dbl_part, "tensor").astype(jnp.bfloat16)
    grad_act = grad_act_scan + dot_last(grad_dbl, xproj_rows)
    grad_xproj_w = dot_first(x_act, grad_dbl)
    grad_x_part, grad_taps, grad_shift = pull_conv(grad_act)
    grad_mixing = (
        jnp.stack([grad_x_part, grad_gate_part], axis=1)
        .reshape(group_rows, 2 * inner_width)
        .astype(jnp.bfloat16)
    )
    grad_mamba_in_w = dot_first(whole_in, grad_mixing).reshape(mamba_in_all.shape)
    grad_in_part = dot_last(grad_qkv, qkv_all) + dot_last(grad_mixing, mamba_in_flat)
    grad_in_rows = lax.psum_scatter(
        grad_in_part.astype(jnp.bfloat16), "tensor", scatter_dimension=0, tiled=True
    ).astype(jnp.float32)
    grad_in_norm, grad_gain_in = pull_in(grad_in_rows)
    grad_inputs = grad_resid + grad_in_norm
    gain_grads = jnp.stack([grad_gain_in, grad_gain_attn, grad_gain_ssm, grad_gain_mid])
    vector_grads = jnp.concatenate([grad_vectors, grad_shift[None, :], grad_taps], axis=0)
    vector_full = place_block(vector_grads, inner_start, inner_all, 1)
    xproj_full = place_block(grad_xproj_w, inner_start, inner_all, 0)
    dtproj_full = place_block(grad_dtproj, inner_start, inner_all, 1)
    (
        qkv_shard,
        out_shard,
        mamba_in_shard,
        mamba_out_shard,
        gains_shard,
        vectors_shard,
        xproj_shard,
        dtproj_shard,
        gate_shard,
        up_shard,
        down_shard,
    ) = (
        lax.psum_scatter(grad_qkv_w, "dp", scatter_dimension=0, tiled=True),
        lax.psum_scatter(grad_out_w, "dp", scatter_dimension=1, tiled=True),
        lax.psum_scatter(grad_mamba_in_w, "dp", scatter_dimension=0, tiled=True),
        lax.psum_scatter(grad_mamba_out_w, "dp", scatter_dimension=1, tiled=True),
        lax.psum_scatter(gain_grads, "dp", scatter_dimension=1, tiled=True),
        lax.psum_scatter(vector_full, "dp", scatter_dimension=1, tiled=True),
        lax.psum_scatter(xproj_full, "dp", scatter_dimension=0, tiled=True),
        lax.psum_scatter(dtproj_full, "dp", scatter_dimension=1, tiled=True),
        lax.psum_scatter(grad_gate_w, "dp", scatter_dimension=0, tiled=True),
        lax.psum_scatter(grad_up_w, "dp", scatter_dimension=0, tiled=True),
        lax.psum_scatter(grad_down_w, "dp", scatter_dimension=1, tiled=True),
    )
    query_full = place_groups(
        qkv_shard[:, :query_width], first_slot, second_slot, group_width, HEADS * HEAD, 1
    )
    key_full = place_groups(
        qkv_shard[:, query_width : query_width + 2 * HEAD],
        first_slot,
        second_slot,
        HEAD,
        KV * HEAD,
        1,
    )
    value_full = place_groups(
        qkv_shard[:, query_width + 2 * HEAD :], first_slot, second_slot, HEAD, KV * HEAD, 1
    )
    out_full = place_groups(out_shard, first_slot, second_slot, group_width, HEADS * HEAD, 0)
    query_sum, key_sum, value_sum, out_sum, gains_sum, vectors_sum, xproj_sum, dtproj_sum = (
        lax.psum(query_full.astype(jnp.bfloat16), "tensor").astype(jnp.float32),
        lax.psum(key_full.astype(jnp.bfloat16), "tensor").astype(jnp.float32),
        lax.psum(value_full.astype(jnp.bfloat16), "tensor").astype(jnp.float32),
        lax.psum(out_full.astype(jnp.bfloat16), "tensor").astype(jnp.float32),
        lax.psum(gains_shard.astype(jnp.bfloat16), "tensor").astype(jnp.float32),
        lax.psum(vectors_shard.astype(jnp.bfloat16), "tensor").astype(jnp.float32),
        lax.psum(xproj_shard.astype(jnp.bfloat16), "tensor").astype(jnp.float32),
        lax.psum(dtproj_shard.astype(jnp.bfloat16), "tensor").astype(jnp.float32),
    )
    return (
        result,
        grad_inputs,
        gains_sum[0],
        query_sum,
        key_sum,
        value_sum,
        out_sum,
        mamba_in_shard,
        vectors_sum[4:],
        vectors_sum[3],
        xproj_sum,
        dtproj_sum,
        vectors_sum[0],
        vectors_sum[1],
        vectors_sum[2],
        mamba_out_shard,
        gains_sum[1],
        gains_sum[2],
        gains_sum[3],
        gate_shard,
        up_shard,
        down_shard,
    )


def solution(mesh):
    placed = (
        P(("dp", "tensor"), None),
        P(("dp", "tensor"), None),
        P("dp"),
        P(("dp", "tensor")),
        P("dp"),
        P("dp", None),
        P("dp", None),
        P("dp", None),
        P(None, "dp"),
        P("dp", None, "tensor"),
        P(None, "dp"),
        P("dp"),
        P("dp", None),
        P(None, "dp"),
        P("dp"),
        P("dp"),
        P("dp"),
        P("tensor", "dp"),
        P("dp"),
        P("dp"),
        P("dp"),
        P("dp", "tensor"),
        P("dp", "tensor"),
        P("tensor", "dp"),
    )
    return jax.shard_map(
        per_device,
        mesh=mesh,
        in_specs=placed,
        out_specs=(
            P(("dp", "tensor"), None),
            P(("dp", "tensor"), None),
            P("dp"),
            P("dp", None),
            P("dp", None),
            P("dp", None),
            P(None, "dp"),
            P("dp", None, "tensor"),
            P(None, "dp"),
            P("dp"),
            P("dp", None),
            P(None, "dp"),
            P("dp"),
            P("dp"),
            P("dp"),
            P("tensor", "dp"),
            P("dp"),
            P("dp"),
            P("dp"),
            P("dp", "tensor"),
            P("dp", "tensor"),
            P("tensor", "dp"),
        ),
        check_vma=False,
    )
```

profile of v0, /device:TPU:17, one launch (start us, length us, event | category | flops | bytes accessed | tf_op | source)
XLA Modules:
  0.0 4656.5 jit_solution(14062659999050523619)
XLA Ops:
  11.5 19.4 all-gather
  43.6 24.6 all-gather.1
  69.3 33.2 all-gather.2
  105.2 27.5 all_gather.58
  142.6 28.4 all-gather.16.cloned.1.call-done
  171.0 16.3 fusion.146
  208.0 28.1 all-reduce.40
  263.3 594.6 %while.151 = (s32[]{:T(128)}, f32[16,800]{1,0:T(8,128)}, s32[]{:T(128)}, f32[32,64,800]{2,1,0:T(8,128)}, f32[32,16,800]{2,1,0:T(8,128)}, /*index=5*/s32[32]{0:T(...) while((s32[]{:T(128)}, f32[16,800]{1,0:T(8,128)}, ...), condition=%wide.region_9.10_spmd.clone, body=%wide.region_8.9_spmd.clone.sunk | while | flops 79987968 | bytes 3377451 | solution.py:238
  901.3 192.0 %while.149 = (s32[]{:T(128)}, bf16[4,512,2,5,64]{1,4,3,2,0:T(8,128)(2,1)}, f32[4,2,5,512,1]{3,2,1,4,0:T(8,128)}, s32[4]{0:T(128)S(1)}, bf16[3072,2,64]{0,2,1:T(8...) while((s32[]{:T(128)}, ...), condition=%wide.region_4.5_spmd, body=%wide.region_1.0_spmd.sunk | while | flops 2112680960 | bytes 99857672 | solution.py:118
  904.7 18.8 fusion.329
  923.6 14.2 fusion.330
  938.4 15.2 fusion.331
  956.9 14.2 fusion.329
  985.6 15.0 fusion.331
  1032.0 14.9 fusion.331
  1078.4 14.9 fusion.331
  1129.1 85.1 %reduce-scatter.27.cloned.1.call-done = f32[512,1600]{0,1:T(8,128)} async-done(((f32[2048,1600]{0,1:T(8,128)}), f32[512,1600]{0,1:T(8,128)}) %reduce-scatter.27.cloned.1.call-update) | async-done | bytes 3276816 | tf_op jit(solution)/shard_map/reduce_scatter | solution.py:392
  1225.3 67.1 %all-gather.28.cloned.1.call-done = bf16[1600,1376]{1,0:T(8,128)(2,1)} async-done(((bf16[200,1376]{1,0:T(8,128)(2,1)}), bf16[1600,1376]{1,0:T(8,128)(2,1)}) %all-gather.28.cloned.1.call-update) | async-done | bytes 4403216 | tf_op jit(solution)/shard_map/all_gather | solution.py:338
  1292.4 49.4 %all-gather.26.cloned.1.call-done = bf16[2048,1600]{0,1:T(8,128)(2,1)} async-done(((bf16[512,1600]{0,1:T(8,128)(2,1)}), bf16[2048,1600]{0,1:T(8,128)(2,1)}) %all-gather.26.cloned.1.call-update) | async-done | bytes 6553616 | tf_op jit(solution)/shard_map/all_gather | solution.py:398
  1341.8 16.3 fusion.213
  1358.1 61.3 %all-gather.30.cloned.1.call-done = bf16[1600,1376]{1,0:T(8,128)(2,1)} async-done(((bf16[200,1376]{1,0:T(8,128)(2,1)}), bf16[1600,1376]{1,0:T(8,128)(2,1)}) %all-gather.30.cloned.1.call-update) | async-done | bytes 4403216 | tf_op jit(solution)/shard_map/all_gather | solution.py:339
  1419.4 20.3 multiply_convert_fusion.2
  1439.7 57.4 %all-gather.32.cloned.1.call-done = bf16[1376,1600]{0,1:T(8,128)(2,1)} async-done(((bf16[1376,200]{0,1:T(8,128)(2,1)}), bf16[1376,1600]{0,1:T(8,128)(2,1)}) %all-gather.32.cloned.1.call-update) | async-done | bytes 4403216 | tf_op jit(solution)/shard_map/all_gather | solution.py:340
  1497.0 16.6 fusion.218
  1515.6 39.2 psum.78
  1555.5 61.0 %reduce-scatter.31.cloned.1.call-done = f32[512,1600]{0,1:T(8,128)} async-done(((f32[2048,1600]{0,1:T(8,128)}), f32[512,1600]{0,1:T(8,128)}) %reduce-scatter.31.cloned.1.call-update) | async-done | bytes 3276816 | tf_op jit(solution)/shard_map/reduce_scatter | solution.py:403
  1623.0 48.4 %all-gather.34.cloned.1.call-done = bf16[2048,1600]{0,1:T(8,128)(2,1)} async-done(((bf16[512,1600]{0,1:T(8,128)(2,1)}), bf16[2048,1600]{0,1:T(8,128)(2,1)}) %all-gather.34.cloned.1.call-update) | async-done | bytes 6553616 | tf_op jit(solution)/shard_map/all_gather | solution.py:409
  1671.3 25.0 multiply_convert_fusion
  1696.3 14.0 fusion.219
  1710.4 17.4 convolution_add_fusion.4
  1728.5 101.6 %reduce-scatter.33.cloned.1.call-done = f32[512,1600]{0,1:T(8,128)} async-done(((f32[2048,1600]{0,1:T(8,128)}), f32[512,1600]{0,1:T(8,128)}) %reduce-scatter.33.cloned.1.call-update) | async-done | bytes 3276816 | tf_op jit(solution)/shard_map/reduce_scatter | solution.py:418
  1844.5 47.8 %all-gather.38.cloned.1.call-done = bf16[2048,1600]{0,1:T(8,128)(2,1)} async-done(((bf16[512,1600]{0,1:T(8,128)(2,1)}), bf16[2048,1600]{0,1:T(8,128)(2,1)}) %all-gather.38.cloned.1.call-update) | async-done | bytes 6553616 | tf_op jit(solution)/shard_map/all_gather | solution.py:429
  1892.3 15.1 multiply_reduce_fusion.8
  1923.6 908.9 %while.152 = (s32[]{:T(128)}, f32[800]{0:T(1024)S(1)}, f32[16,800]{1,0:T(8,128)S(1)}, f32[32,64,800]{2,1,0:T(8,128)}, f32[32,64,800]{2,1,0:T(8,128)}, /*index=5*...) while((s32[]{:T(128)}, f32[800]{0:T(1024)S(1)}, ...), condition=%wide.region_29.30_spmd.clone, body=%wide.region_23.29_spmd.clone.sunk | while | flops 191140384 | bytes 10556594 | solution.py:238
  2861.0 28.5 all-reduce.41
  2913.1 427.3 %while.150 = (s32[]{:T(128)}, f32[3072,2,64]{0,2,1:T(8,128)}, f32[3072,2,64]{0,2,1:T(8,128)}, bf16[4,512,2,5,64]{1,4,3,2,0:T(8,128)(2,1)}, s32[4]{0:T(128)S(1)},...) while((s32[]{:T(128)}, f32[3072,2,64]{0,2,1:T(8,128)}, ...), condition=%wide.region_21.22_spmd, body=%wide.region_19.21_spmd.sunk | while | flops 5156762624 | bytes 247518064 | solution.py:177
  2932.9 25.8 fusion.342
  2958.7 26.6 fusion.343
  3006.5 14.4 fusion.345
  3040.4 25.6 fusion.342
  3065.9 26.2 fusion.343
  3112.8 14.4 fusion.345
  3146.7 25.6 fusion.342
  3172.3 26.2 fusion.343
  3219.2 14.4 fusion.345
  3253.2 25.6 fusion.342
  3278.7 26.2 fusion.343
  3325.6 14.3 fusion.345
  3374.2 28.6 multiply_reduce_fusion.6
  3415.2 14.0 fusion.134
  3442.6 230.9 %all-reduce.37.cloned.1.call-done = (f32[1600,896]{1,0:T(8,128)}, f32[640,1600]{0,1:T(8,128)}) async-done(((f32[1600,896]{1,0:T(8,128)}, f32[640,1600]{0,1:T(8,128)}), (f32[1600,896]{1,0:T(8,128)}, f32[640,1600]{0,1:T(8,128)})) %all-reduce.37.cloned.1.call-update) | async-done | bytes 9830416
  3700.9 19.8 fusion.125
  3722.7 17.0 fusion.135
  3739.8 15.7 fusion.217
  3755.6 16.1 fusion.215
  3771.7 15.8 fusion.216
  3812.8 44.6 reduce-scatter.35.cloned.1.call-done
  3860.2 30.3 all-reduce.22
  3890.5 17.9 all-reduce.30
  3915.7 137.6 %reduce-scatter.37.cloned.1.call-done = f32[200,2,800]{2,0,1:T(8,128)} async-done(((f32[1600,2,800]{2,0,1:T(8,128)}), f32[200,2,800]{2,0,1:T(8,128)}) %reduce-scatter.37.cloned.1.call-update) | async-done | bytes 1280016 | tf_op jit(solution)/shard_map/reduce_scatter | solution.py:496
  4056.5 157.5 %reduce-scatter.51.cloned.1.call-done = f32[1376,200]{0,1:T(8,128)} async-done(((f32[1376,1600]{0,1:T(8,128)}), f32[1376,200]{0,1:T(8,128)}) %reduce-scatter.51.cloned.1.call-update) | async-done | bytes 1100816
  4214.1 161.3 %reduce-scatter.47.cloned.1.call-done = f32[200,1376]{1,0:T(8,128)} async-done(((f32[1600,1376]{1,0:T(8,128)}), f32[200,1376]{1,0:T(8,128)}) %reduce-scatter.47.cloned.1.call-update) | async-done | bytes 1100816
  4375.4 160.7 %reduce-scatter.49.cloned.1.call-done = f32[200,1376]{1,0:T(8,128)} async-done(((f32[1600,1376]{1,0:T(8,128)}), f32[200,1376]{1,0:T(8,128)}) %reduce-scatter.49.cloned.1.call-update) | async-done | bytes 1100816
  4536.1 113.1 %reduce-scatter.45.cloned.1.call-done = f32[800,200]{0,1:T(8,128)} async-done(((f32[800,1600]{0,1:T(8,128)}), f32[800,200]{0,1:T(8,128)}) %reduce-scatter.45.cloned.1.call-update) | async-done | bytes 640016
  (2056 shorter events, 2030.9 us)
Async XLA Ops:
  7.2 28.0 copy-start.4
  7.2 126.3 %all-gather.22.cloned.1.call-start = ((), (), s32[]{:S(2)}) async-start(), calls=%async_computation.17 | async-start | bytes 6451200 | tf_op jit(solution)/shard_map/all_gather | solution.py:332
  9.5 161.6 %all-gather.16.cloned.1.call-start = ((), (), s32[]{:S(2)}) async-start(), calls=%async_computation.13 | async-start | bytes 8192000 | tf_op jit(solution)/shard_map/all_gather | solution.py:348
  31.7 37.6 copy-start.36
  36.7 68.5 %copy-start.41 = (bf16[100,400]{0,1:T(8,128)(2,1)S(1)}, bf16[100,400]{0,1:T(8,128)(2,1)}, u32[]{:S(2)}) copy-start(bf16[100,400]{0,1:T(8,128)(2,1)} %param.45) | copy-start | bytes 240004
  36.7 829.4 %all-gather.18.cloned.1.call-start = ((), (), s32[]{:S(2)}) async-start(), calls=%async_computation.14 | async-start | bytes 3225600 | tf_op jit(solution)/shard_map/all_gather | solution.py:330
  40.1 847.1 %all-gather.24.cloned.1.call-start = ((), (), s32[]{:S(2)}) async-start(), calls=%async_computation.18 | async-start | bytes 3225600 | tf_op jit(solution)/shard_map/all_gather | solution.py:333
  40.6 1059.7 %all-gather.20.cloned.1.call-start = ((), (), s32[]{:S(2)}) async-start(), calls=%async_computation.15 | async-start | bytes 2304000 | tf_op jit(solution)/shard_map/all_gather | solution.py:331
  42.7 1082.8 %reduce-scatter.29.cloned.1.call-start = ((), (), s32[]{:S(2)}) async-start(), calls=%async_computation.19 | async-start | bytes 16384000 | tf_op jit(solution)/shard_map/reduce_scatter | solution.py:393
  69.1 122.8 %copy-start.76 = (f32[800]{0:T(1024)}, f32[800]{0:T(1024)S(1)}, u32[]{:S(2)}) copy-start(f32[800]{0:T(1024)S(1)} %get-tuple-element.1486) | copy-start | bytes 9604
  69.1 122.8 %copy-start.78 = (f32[800]{0:T(1024)}, f32[800]{0:T(1024)S(1)}, u32[]{:S(2)}) copy-start(f32[800]{0:T(1024)S(1)} %get-tuple-element.1487) | copy-start | bytes 9604
  69.1 122.8 %copy-start.80 = (f32[800]{0:T(1024)}, f32[800]{0:T(1024)S(1)}, u32[]{:S(2)}) copy-start(f32[800]{0:T(1024)S(1)} %get-tuple-element.1488) | copy-start | bytes 9604
  69.1 122.8 %copy-start.82 = (f32[800]{0:T(1024)}, f32[800]{0:T(1024)S(1)}, u32[]{:S(2)}) copy-start(f32[800]{0:T(1024)S(1)} %get-tuple-element.1489) | copy-start | bytes 9604
  69.1 168.7 %copy-start.73 = (f32[800]{0:T(1024)}, f32[800]{0:T(1024)S(1)}, u32[]{:S(2)}) copy-start(f32[800]{0:T(1024)S(1)} %get-tuple-element.1485) | copy-start | bytes 9604
  69.3 122.7 %copy-start.55 = (f32[1,2048]{1,0:T(1,128)}, f32[1,2048]{1,0:T(1,128)S(1)}, u32[]{:S(2)}) copy-start(f32[1,2048]{1,0:T(1,128)S(1)} %get-tuple-element.1661) | copy-start | bytes 24580
  69.3 122.7 %copy-start.57 = (f32[1,2048]{1,0:T(1,128)}, f32[1,2048]{1,0:T(1,128)S(1)}, u32[]{:S(2)}) copy-start(f32[1,2048]{1,0:T(1,128)S(1)} %get-tuple-element.1662) | copy-start | bytes 24580
  69.3 122.7 %copy-start.59 = (f32[1,2048]{1,0:T(1,128)}, f32[1,2048]{1,0:T(1,128)S(1)}, u32[]{:S(2)}) copy-start(f32[1,2048]{1,0:T(1,128)S(1)} %get-tuple-element.1663) | copy-start | bytes 24580
  200.1 680.4 %copy-start = (bf16[1,2048,800]{1,2,0:T(8,128)(2,1)}, bf16[1,2048,800]{1,2,0:T(8,128)(2,1)S(1)}, u32[]{:S(2)}) copy-start(bf16[1,2048,800]{1,2,0:T(8,128)(2,1)S(1)} %get-tuple-element.1617) | copy-start | bytes 9830404
  299.7 17.3 copy-start.97
  411.3 17.3 copy-start.97
  448.6 17.3 copy-start.97
  783.5 17.3 copy-start.97
  820.7 17.3 copy-start.97
  899.4 314.9 %reduce-scatter.27.cloned.1.call-start = ((), (), s32[]{:S(2)}) async-start(), calls=%async_computation.16 | async-start | bytes 16384000 | tf_op jit(solution)/shard_map/reduce_scatter | solution.py:392
  1093.3 17.4 copy-start.10
  1093.3 17.4 copy-start.25
  1110.8 106.3 %copy-start.5 = (f32[512,1600]{0,1:T(8,128)S(1)}, f32[512,1600]{0,1:T(8,128)}, u32[]{:S(2)}) copy-start(f32[512,1600]{0,1:T(8,128)} %param.32) | copy-start | bytes 9830404
  1110.8 106.2 %copy-start.42 = (f32[1600]{0:T(1024)S(1)}, f32[1600]{0:T(1024)}, u32[]{:S(2)}) copy-start(f32[1600]{0:T(1024)} %get-tuple-element.1491) | copy-start | bytes 19204
  1110.8 106.2 %copy-start.44 = (f32[1600]{0:T(1024)S(1)}, f32[1600]{0:T(1024)}, u32[]{:S(2)}) copy-start(f32[1600]{0:T(1024)} %get-tuple-element.1492) | copy-start | bytes 19204
  1110.8 181.6 %all-gather.28.cloned.1.call-start = ((), (), s32[]{:S(2)}) async-start(), calls=%async_computation.21 | async-start | bytes 5068800 | tf_op jit(solution)/shard_map/all_gather | solution.py:338
  1111.6 230.2 %all-gather.26.cloned.1.call-start = ((), (), s32[]{:S(2)}) async-start(), calls=%async_computation.20 | async-start | bytes 8192000 | tf_op jit(solution)/shard_map/all_gather | solution.py:398
  1125.5 95.7 %copy-start.39 = (f32[1600]{0:T(1024)}, f32[1600]{0:T(1024)S(1)}, u32[]{:S(2)}) copy-start(f32[1600]{0:T(1024)S(1)} %convert_element_type.234) | copy-start | bytes 19204
  1129.1 91.5 %copy-start.61 = (f32[512]{0:T(512)}, f32[512]{0:T(512)S(1)}, u32[]{:S(2)}) copy-start(f32[512]{0:T(512)S(1)} %fusion.194) | copy-start | bytes 6148
  1223.9 195.5 %all-gather.30.cloned.1.call-start = ((), (), s32[]{:S(2)}) async-start(), calls=%async_computation.22 | async-start | bytes 5068800 | tf_op jit(solution)/shard_map/all_gather | solution.py:339
  1224.5 272.5 %all-gather.32.cloned.1.call-start = ((), (), s32[]{:S(2)}) async-start(), calls=%async_computation.23 | async-start | bytes 5068800 | tf_op jit(solution)/shard_map/all_gather | solution.py:340
  1225.2 391.2 %reduce-scatter.31.cloned.1.call-start = ((), (), s32[]{:S(2)}) async-start(), calls=%async_computation.24 | async-start | bytes 16384000 | tf_op jit(solution)/shard_map/reduce_scatter | solution.py:403
  1513.6 102.8 %copy-start.8 = (f32[512,1600]{0,1:T(8,128)S(1)}, f32[512,1600]{0,1:T(8,128)}, u32[]{:S(2)}) copy-start(f32[512,1600]{0,1:T(8,128)} %copy-done.7) | copy-start | bytes 9830404
  1513.6 157.7 %all-gather.34.cloned.1.call-start = ((), (), s32[]{:S(2)}) async-start(), calls=%async_computation.25 | async-start | bytes 8192000 | tf_op jit(solution)/shard_map/all_gather | solution.py:409
  1622.9 207.2 %reduce-scatter.33.cloned.1.call-start = ((), (), s32[]{:S(2)}) async-start(), calls=%async_computation.26 | async-start | bytes 16384000 | tf_op jit(solution)/shard_map/reduce_scatter | solution.py:418
  1727.8 102.3 %copy-start.40 = (f32[1600]{0:T(1024)S(1)}, f32[1600]{0:T(1024)}, u32[]{:S(2)}) copy-start(f32[1600]{0:T(1024)} %copy-done.39) | copy-start | bytes 19204
  1727.8 102.3 %copy-start.51 = (f32[512]{0:T(512)S(1)}, f32[512]{0:T(512)}, u32[]{:S(2)}) copy-start(f32[512]{0:T(512)} %copy-done.50) | copy-start | bytes 6148
  1727.8 105.8 %copy-start.66 = (f32[512]{0:T(512)S(1)}, f32[512]{0:T(512)}, u32[]{:S(2)}) copy-start(f32[512]{0:T(512)} %copy-done.65) | copy-start | bytes 6148
  1727.8 105.8 %copy-start.62 = (f32[512]{0:T(512)S(1)}, f32[512]{0:T(512)}, u32[]{:S(2)}) copy-start(f32[512]{0:T(512)} %copy-done.61) | copy-start | bytes 6148
  1727.8 105.8 %copy-start.64 = (f32[512]{0:T(512)S(1)}, f32[512]{0:T(512)}, u32[]{:S(2)}) copy-start(f32[512]{0:T(512)} %copy-done.63) | copy-start | bytes 6148
  1727.8 164.5 %all-gather.38.cloned.1.call-start = ((), (), s32[]{:S(2)}) async-start(), calls=%async_computation.28 | async-start | bytes 8192000 | tf_op jit(solution)/shard_map/all_gather | solution.py:429
  1840.6 51.7 %copy-start.1 = (bf16[1,2048,800]{1,2,0:T(8,128)(2,1)S(1)}, bf16[1,2048,800]{1,2,0:T(8,128)(2,1)}, u32[]{:S(2)}) copy-start(bf16[1,2048,800]{1,2,0:T(8,128)(2,1)} %copy-done) | copy-start | bytes 9830404
  1843.9 1056.3 %all-gather.36.cloned.1.call-start = ((), (), s32[]{:S(2)}) async-start(), calls=%async_computation.27 | async-start | bytes 8192000 | tf_op jit(solution)/shard_map/all_gather | solution.py:428
  1844.5 1594.7 %reduce-scatter.39.cloned.1.call-start = ((), (), s32[]{:S(2)}) async-start(), calls=%async_computation.31 | async-start | bytes 1843200 | tf_op jit(solution)/shard_map/reduce_scatter | solution.py:501
  2855.8 33.8 copy-start.2
  2861.0 579.8 %reduce-scatter.43.cloned.1.call-start = ((), (), s32[]{:S(2)}) async-start(), calls=%async_computation.33 | async-start | bytes 3686400
  2910.3 763.2 %all-reduce.37.cloned.1.call-start = ((), (), s32[]{:S(2)}) async-start(), calls=%async_computation.38 | async-start | bytes 19660800
  3364.8 435.5 %reduce-scatter.41.cloned.1.call-start = ((), (), s32[]{:S(2)}) async-start(), calls=%async_computation.32 | async-start | bytes 1843200
  3374.1 31.1 copy-start.3
  3415.1 386.4 %all-reduce.39.cloned.1.call-start = ((), (), s32[]{:S(2)}) async-start(), calls=%async_computation.39 | async-start | bytes 3760128 | tf_op jit(solution)/shard_map/psum | solution.py:522
  3700.9 156.5 %reduce-scatter.35.cloned.1.call-start = ((), (), s32[]{:S(2)}) async-start(), calls=%async_computation.29 | async-start | bytes 8192000 | tf_op jit(solution)/shard_map/reduce_scatter | solution.py:471
  3720.8 332.5 %reduce-scatter.37.cloned.1.call-start = ((), (), s32[]{:S(2)}) async-start(), calls=%async_computation.30 | async-start | bytes 12902400 | tf_op jit(solution)/shard_map/reduce_scatter | solution.py:496
  3739.7 474.3 %reduce-scatter.51.cloned.1.call-start = ((), (), s32[]{:S(2)}) async-start(), calls=%async_computation.37 | async-start | bytes 10137600
  3755.5 619.9 %reduce-scatter.47.cloned.1.call-start = ((), (), s32[]{:S(2)}) async-start(), calls=%async_computation.35 | async-start | bytes 10137600
  3771.7 764.4 %reduce-scatter.49.cloned.1.call-start = ((), (), s32[]{:S(2)}) async-start(), calls=%async_computation.36 | async-start | bytes 10137600
  3787.6 861.6 %reduce-scatter.45.cloned.1.call-start = ((), (), s32[]{:S(2)}) async-start(), calls=%async_computation.34 | async-start | bytes 6451200
  3800.2 57.2 %copy-start.6 = (f32[512,1600]{0,1:T(8,128)S(1)}, f32[512,1600]{0,1:T(8,128)}, u32[]{:S(2)}) copy-start(f32[512,1600]{0,1:T(8,128)} %param.32) | copy-start | bytes 9830404
  3800.2 57.2 %copy-start.38 = (f32[1600]{0:T(1024)S(1)}, f32[1600]{0:T(1024)}, u32[]{:S(2)}) copy-start(f32[1600]{0:T(1024)} %copy-done.37) | copy-start | bytes 19204
  3800.2 57.2 %copy-start.49 = (f32[512]{0:T(512)S(1)}, f32[512]{0:T(512)}, u32[]{:S(2)}) copy-start(f32[512]{0:T(512)} %copy-done.48) | copy-start | bytes 6148
  3800.2 109.4 %copy-start.68 = (f32[512]{0:T(512)S(1)}, f32[512]{0:T(512)}, u32[]{:S(2)}) copy-start(f32[512]{0:T(512)} %copy-done.67) | copy-start | bytes 6148
  (128 other events, 947.9 us)
Sparse Core Ops, SparseCore 0:
  10.8 110.3 all-gather.21
  123.4 47.6 all-gather.15
  173.8 56.0 all-gather.17
  232.0 55.9 all-gather.23
  290.6 47.5 all-gather.19
  899.5 103.2 reduce-scatter.28
  1110.9 103.2 reduce-scatter.26
  1216.4 75.9 all-gather.27
  1293.9 47.7 all-gather.25
  1343.8 75.5 all-gather.29
  1421.5 75.4 all-gather.31
  1513.8 102.6 reduce-scatter.30
  1623.0 48.2 all-gather.33
  1727.9 102.0 reduce-scatter.32
  1844.0 48.2 all-gather.37
  1893.7 47.8 all-gather.35
  2861.1 62.8 reduce-scatter.38
  2927.9 76.1 reduce-scatter.42
  3364.9 308.5 all-reduce.36
  3677.1 63.0 reduce-scatter.40
  3744.2 50.0 all-reduce.38
  3797.0 60.3 reduce-scatter.34
  3861.0 192.3 reduce-scatter.36
  4057.3 156.7 reduce-scatter.50
  4218.6 156.7 reduce-scatter.46
  4379.3 156.7 reduce-scatter.48
  4540.4 108.7 reduce-scatter.44
where the time goes:
time: 4680 us; the launch traced here: 4660 us
  waiting for transfers between devices  1620 us (35%)
  other arithmetic  1180 us (25%)
  matrix products  1080 us (23%)
  local copies, waits for them, and re-layouts  399 us (9%)
  blocking collectives  261 us (6%)
  loops' own time  104 us (2%)
    unnamed x34, waiting for transfers between devices  827 us
    dot_general x64, other arithmetic, stretch_step(): jnp.einsum('tsc,ts,sc->tc', transfer, gram_matrix, drive_term, precision=...  356 us
    reduce_sum x32, other arithmetic, stretch_step(): cumulated[:, None, :] - cumulated[None, :, :]  316 us
    dot_general x8, matrix products, dot_last(): lax.dot_general(left, right, (((1,), (1,)), ((), ())), preferred_element_...  138 us
    reduce_scatter x1, waiting for transfers between devices, per_device(): lax.psum_scatter(grad_mamba_in_w, 'dp', scatter_dimension=0, tiled=True)  138 us
    squeeze x160, local copies, waits for them, and re-layouts, scan_sequence(): lax.scan(lambda carry_state, piece: stepper(carry_state, piece, decay_rat...  137 us
    dot_general x8, matrix products, one_block(): jnp.einsum('qgjd,kgd->gjqk', query_blk, key_blk, preferred_element_type=j...  115 us
    dot_general x8, matrix products, dot_plain(): return jnp.dot(left, right, preferred_element_type=jnp.float32)  105 us
  transfers between devices with their start and end apart: 27, of which 17 were waited for; matrix products, arithmetic and copies ran while one was open for 54% of the time, Pallas kernels for 0%

commit v1 on v0

v1 whole, which is shorter than its diff:
```python
import functools

import jax
import jax.numpy as jnp
from jax import lax
from jax.experimental import pallas as pl
from jax.experimental.pallas import tpu as pltpu
from jax.sharding import PartitionSpec as P

HEADS = 25
KV = 5
HEAD = 64
STATE = 16
RANK = 100
CONV = 4
WINDOW = 1024
BLOCK = 512
STRETCH = 64
LEN = 2048


EPSILON = 1e-06
MASKED = -1e30
HIGHEST = lax.Precision.HIGHEST


def normalize_t(values, gain):
    return values * lax.rsqrt(jnp.mean(values * values, axis=0, keepdims=True) + EPSILON) * gain


def join_rows_t(resid, attn_sum, ssm_sum, gain_attn, gain_ssm):
    return resid + 0.5 * (normalize_t(attn_sum, gain_attn) + normalize_t(ssm_sum, gain_ssm))


def dot_plain(left, right):
    return jnp.dot(left, right, preferred_element_type=jnp.float32)


def dot_last(left, right):
    return lax.dot_general(
        left, right, (((1,), (1,)), ((), ())), preferred_element_type=jnp.float32
    )


def dot_first(left, right):
    return lax.dot_general(
        left, right, (((0,), (0,)), ((), ())), preferred_element_type=jnp.float32
    )


def pick_groups(weight, first_slot, second_slot, group_width, axis):
    return jnp.concatenate(
        [
            lax.dynamic_slice_in_dim(weight, first_slot * group_width, group_width, axis),
            lax.dynamic_slice_in_dim(weight, second_slot * group_width, group_width, axis),
        ],
        axis=axis,
    )


PIECES = 4
MESH = pl.DeviceIdType.MESH


def tensor_peers():
    me = lax.axis_index("tensor")
    side = me + 1 - 2 * lax.rem(me, 2)
    cross = lax.rem(me + 2, 4)
    return me, side, cross, lax.rem(side + 2, 4)


def greet(peers):
    barrier = pltpu.get_barrier_semaphore()
    for peer in peers:
        pl.semaphore_signal(barrier, inc=1, device_id={"tensor": peer}, device_id_type=MESH)
    pl.semaphore_wait(barrier, len(peers))


def push(src, dst, sems, index, peer):
    copy = pltpu.make_async_remote_copy(
        src_ref=src,
        dst_ref=dst,
        send_sem=sems[0].at[index],
        recv_sem=sems[1].at[index],
        device_id={"tensor": peer},
        device_id_type=MESH,
    )
    copy.start()
    return copy


def columns(block, size):
    return pl.ds(pl.multiple_of(block * size, size), size)


def gather_kernel(part_ref, whole_ref, own_sem, *sems):
    me, side, cross, diag = tensor_peers()
    depth, size = part_ref.shape
    step = depth // PIECES
    mine = columns(me, size)
    theirs = columns(cross, size)
    greet((side, cross))
    own = pltpu.make_async_copy(part_ref, whole_ref.at[:, mine], own_sem)
    own.start()
    over, near, relay = [], [], []
    for piece in range(PIECES):
        rows = pl.ds(piece * step, step)
        over.append(
            push(part_ref.at[rows], whole_ref.at[rows, mine], sems[0:2], piece, cross)
        )
    for piece in range(PIECES):
        rows = pl.ds(piece * step, step)
        near.append(push(part_ref.at[rows], whole_ref.at[rows, mine], sems[2:4], piece, side))
    for piece in range(PIECES):
        rows = pl.ds(piece * step, step)
        over[piece].wait_recv()
        relay.append(
            push(whole_ref.at[rows, theirs], whole_ref.at[rows, theirs], sems[4:6], piece, side)
        )
    own.wait()
    for piece in range(PIECES):
        over[piece].wait_send()
        near[piece].wait()
        relay[piece].wait()


def gather_rows(part, call_id):
    depth, size = part.shape
    return pl.pallas_call(
        gather_kernel,
        name="gather_rows",
        in_specs=[pl.BlockSpec(memory_space=pl.ANY)],
        out_specs=pl.BlockSpec(memory_space=pl.ANY),
        out_shape=jax.ShapeDtypeStruct((depth, 4 * size), part.dtype),
        scratch_shapes=[pltpu.SemaphoreType.DMA] + [pltpu.SemaphoreType.DMA((PIECES,))] * 6,
        compiler_params=pltpu.CompilerParams(
            collective_id=call_id, has_side_effects=True, vmem_limit_bytes=1 << 20
        ),
        cost_estimate=pl.CostEstimate(
            flops=0, bytes_accessed=depth * size * 2 * 90, transcendentals=0
        ),
    )(part)


def reduce_kernel(part_ref, out_ref, near_buf, own_buf, stage_buf, far_buf, *sems):
    me, side, cross, diag = tensor_peers()
    depth, size = out_ref.shape
    step = depth // PIECES
    greet((side, cross))
    first, second, third = [], [], []
    for piece in range(PIECES):
        rows = pl.ds(piece * step, step)
        first.append(
            push(part_ref.at[rows, columns(diag, size)], near_buf.at[rows], sems[0:2], piece, side)
        )
    for piece in range(PIECES):
        rows = pl.ds(piece * step, step)
        second.append(
            push(part_ref.at[rows, columns(side, size)], own_buf.at[rows], sems[2:4], piece, side)
        )
    for piece in range(PIECES):
        rows = pl.ds(piece * step, step)
        first[piece].wait_recv()
        stage_buf[rows] = (
            part_ref[rows, columns(cross, size)].astype(jnp.float32)
            + near_buf[rows].astype(jnp.float32)
        ).astype(jnp.bfloat16)
        third.append(push(stage_buf.at[rows], far_buf.at[rows], sems[4:6], piece, cross))
    for piece in range(PIECES):
        rows = pl.ds(piece * step, step)
        second[piece].wait_recv()
        out_ref[rows] = part_ref[rows, columns(me, size)].astype(jnp.float32) + own_buf[
            rows
        ].astype(jnp.float32)
    for piece in range(PIECES):
        rows = pl.ds(piece * step, step)
        third[piece].wait_recv()
        out_ref[rows] += far_buf[rows].astype(jnp.float32)
    for piece in range(PIECES):
        first[piece].wait_send()
        second[piece].wait_send()
        third[piece].wait_send()


def reduce_rows(part, call_id):
    depth, total = part.shape
    size = total // 4
    whole = pl.BlockSpec(memory_space=pltpu.VMEM)
    return pl.pallas_call(
        reduce_kernel,
        name="reduce_rows",
        in_specs=[whole],
        out_specs=whole,
        out_shape=jax.ShapeDtypeStruct((depth, size), jnp.float32),
        scratch_shapes=[pltpu.VMEM((depth, size), jnp.bfloat16)] * 4
        + [pltpu.SemaphoreType.DMA((PIECES,))] * 6,
        compiler_params=pltpu.CompilerParams(
            collective_id=call_id, has_side_effects=True, vmem_limit_bytes=32 << 20
        ),
        cost_estimate=pl.CostEstimate(
            flops=0, bytes_accessed=depth * size * 2 * 90, transcendentals=0
        ),
    )(part)


def total_kernel(part_ref, out_ref, near_buf, own_buf, stage_buf, far_buf, low_buf, own_sem, *sems):
    me, side, cross, diag = tensor_peers()
    size, wide = low_buf.shape
    half = size // 2
    greet((side, cross))
    rows_of = lambda block, at: pl.ds(pl.multiple_of(block * size + at, half), half)
    pieces = (0, half)
    first = [
        push(part_ref.at[rows_of(diag, at)], near_buf.at[pl.ds(at, half)], sems[0:2], i, side)
        for i, at in enumerate(pieces)
    ]
    second = [
        push(part_ref.at[rows_of(side, at)], own_buf.at[pl.ds(at, half)], sems[2:4], i, side)
        for i, at in enumerate(pieces)
    ]
    third, over, near, relay = [], [], [], []
    for i, at in enumerate(pieces):
        rows = pl.ds(at, half)
        first[i].wait_recv()
        stage_buf[rows] = (part_ref[rows_of(cross, at)] + near_buf[rows]).astype(jnp.bfloat16)
        third.append(push(stage_buf.at[rows], far_buf.at[rows], sems[4:6], i, cross))
    for i, at in enumerate(pieces):
        rows = pl.ds(at, half)
        second[i].wait_recv()
        third[i].wait_recv()
        low_buf[rows] = (
            part_ref[rows_of(me, at)] + own_buf[rows] + far_buf[rows].astype(jnp.float32)
        ).astype(jnp.bfloat16)
        over.append(push(low_buf.at[rows], out_ref.at[rows_of(me, at)], sems[6:8], i, cross))
        near.append(push(low_buf.at[rows], out_ref.at[rows_of(me, at)], sems[8:10], i, side))
    own = pltpu.make_async_copy(
        low_buf, out_ref.at[pl.ds(pl.multiple_of(me * size, size), size)], own_sem
    )
    own.start()
    for i, at in enumerate(pieces):
        over[i].wait_recv()
        relay.append(
            push(out_ref.at[rows_of(cross, at)], out_ref.at[rows_of(cross, at)], sems[10:12], i, side)
        )
    own.wait()
    for i in range(2):
        for group in (first, second, third, over):
            group[i].wait_send()
        near[i].wait()
        relay[i].wait()


def total_rows(part, call_id):
    tokens, wide = part.shape
    size = tokens // 4
    whole = pl.BlockSpec(memory_space=pltpu.VMEM)
    return pl.pallas_call(
        total_kernel,
        name="total_rows",
        in_specs=[whole],
        out_specs=whole,
        out_shape=jax.ShapeDtypeStruct((tokens, wide), jnp.bfloat16),
        scratch_shapes=[
            pltpu.VMEM((size, wide), jnp.float32),
            pltpu.VMEM((size, wide), jnp.float32),
            pltpu.VMEM((size, wide), jnp.bfloat16),
            pltpu.VMEM((size, wide), jnp.bfloat16),
            pltpu.VMEM((size, wide), jnp.bfloat16),
            pltpu.SemaphoreType.DMA,
        ]
        + [pltpu.SemaphoreType.DMA((2,))] * 12,
        compiler_params=pltpu.CompilerParams(
            collective_id=call_id, has_side_effects=True, vmem_limit_bytes=32 << 20
        ),
        cost_estimate=pl.CostEstimate(flops=0, bytes_accessed=60 << 20, transcendentals=0),
    )(part)


def hello_kernel(gain_ref, count_ref, gains_ref, counts_ref, sum_buf, local_buf, *sems):
    me = lax.axis_index("tensor")
    place = lax.axis_index("dp")
    ranks, groups = local_buf.shape[0], gains_ref.shape[0]
    barrier = pltpu.get_barrier_semaphore()
    others = [{"tensor": lax.rem(me + hop, ranks)} for hop in range(1, ranks)]
    far = [{"dp": lax.rem(place + hop, groups)} for hop in range(1, groups)]
    for peer in others + far:
        pl.semaphore_signal(barrier, inc=1, device_id=peer, device_id_type=MESH)
    pl.semaphore_wait(barrier, len(others) + len(far))

    def send(src, dst, index, peer):
        copy = pltpu.make_async_remote_copy(
            src_ref=src,
            dst_ref=dst,
            send_sem=sems[0].at[index],
            recv_sem=sems[1].at[index],
            device_id=peer,
            device_id_type=MESH,
        )
        copy.start()
        return copy

    first = [send(count_ref, local_buf.at[me], i, peer) for i, peer in enumerate(others)]
    local_buf[me] = count_ref[...]
    gains_ref[place] = gain_ref[...]
    base = len(first)
    second = [send(gain_ref, gains_ref.at[place], base + i, peer) for i, peer in enumerate(far)]
    base += len(second)
    for copy in first:
        copy.wait()
    sum_buf[...] = jnp.sum(local_buf[...], axis=0)
    counts_ref[place] = sum_buf[...]
    third = [send(sum_buf, counts_ref.at[place], base + i, peer) for i, peer in enumerate(far)]
    for copy in second + third:
        copy.wait()


def hello(gains, count):
    wide = -(-gains.shape[1] // 128) * 128
    block = jnp.zeros((8, wide), jnp.float32)
    block = lax.dynamic_update_slice(block, gains.astype(jnp.float32), (0, 0))
    counts = jnp.full((8, 128), count, jnp.float32)
    groups, ranks = lax.axis_size("dp"), lax.axis_size("tensor")
    copies = ranks - 1 + 2 * (groups - 1)
    whole = pl.BlockSpec(memory_space=pltpu.VMEM)
    gains_all, counts_all = pl.pallas_call(
        hello_kernel,
        name="hello",
        in_specs=[whole, whole],
        out_specs=[whole, whole],
        out_shape=[
            jax.ShapeDtypeStruct((groups, 8, wide), jnp.float32),
            jax.ShapeDtypeStruct((groups, 8, 128), jnp.float32),
        ],
        scratch_shapes=[
            pltpu.VMEM((8, 128), jnp.float32),
            pltpu.VMEM((ranks, 8, 128), jnp.float32),
        ]
        + [pltpu.SemaphoreType.DMA((copies,))] * 2,
        compiler_params=pltpu.CompilerParams(collective_id=0, has_side_effects=True),
        cost_estimate=pl.CostEstimate(flops=0, bytes_accessed=30 << 20, transcendentals=0),
    )(block, counts)
    gains_full = gains_all[:, :4, : gains.shape[1]].transpose(1, 0, 2).reshape(4, -1)
    return gains_full, jnp.sum(counts_all[:, 0, 0])


TILE = 400


def weights_kernel(plan, *refs):
    out_ref = refs[-1]
    index = 0
    for mode, offset, size, pad in plan:
        left = refs[index][...]
        if mode == "copy":
            product = left
            index += 1
        else:
            right = refs[index + 1][...]
            product = dot_last(left, right) if mode == "flip" else dot_plain(left, right)
            index += 2
        out_ref[:, offset : offset + size] = product.astype(jnp.bfloat16)
        if pad:
            out_ref[:, offset + size : offset + size + pad] = jnp.zeros(
                (out_ref.shape[0], pad), jnp.bfloat16
            )


def weight_grads(pairs, name, micros, widen=0):
    rows = pairs[0][0].shape[0]
    tile = TILE if rows % TILE == 0 else rows
    plan, specs, operands, offset = [], [], [], 0
    for left, right, flip in pairs:
        source = left if right is None else right
        size = source.shape[0] if flip else source.shape[1]
        pad = -size % 128 + (widen if len(plan) + 1 == len(pairs) else 0)
        mode = "copy" if right is None else "flip" if flip else "plain"
        plan.append((mode, offset, size, pad))
        offset += size + pad
        specs.append(pl.BlockSpec((tile, left.shape[1]), lambda i: (i, 0)))
        operands.append(left)
        if right is not None:
            specs.append(
                pl.BlockSpec(right.shape, lambda i: (0, 0), pipeline_mode=pl.Buffered(1))
            )
            operands.append(right)
    return pl.pallas_call(
        functools.partial(weights_kernel, plan),
        name=name,
        grid=(rows // tile,),
        in_specs=specs,
        out_specs=pl.BlockSpec((tile, offset), lambda i: (i, 0)),
        out_shape=jax.ShapeDtypeStruct((rows, offset), jnp.bfloat16),
        compiler_params=pltpu.CompilerParams(vmem_limit_bytes=52 << 20),
        cost_estimate=pl.CostEstimate(
            flops=0, bytes_accessed=int(micros * 3.6) << 20, transcendentals=0
        ),
    )(*operands)


def farewell_kernel(part_ref, out_ref, group_buf, sum_buf, rank_buf, *sems):
    me = lax.axis_index("tensor")
    place = lax.axis_index("dp")
    ranks, groups = rank_buf.shape[0], group_buf.shape[0]
    barrier = pltpu.get_barrier_semaphore()
    others = [lax.rem(me + hop, ranks) for hop in range(1, ranks)]
    far = [lax.rem(place + hop, groups) for hop in range(1, groups)]
    for peer in others:
        pl.semaphore_signal(barrier, inc=1, device_id={"tensor": peer}, device_id_type=MESH)
    for peer in far:
        pl.semaphore_signal(barrier, inc=1, device_id={"dp": peer}, device_id_type=MESH)
    pl.semaphore_wait(barrier, len(others) + len(far))

    def send(src, dst, index, peer):
        copy = pltpu.make_async_remote_copy(
            src_ref=src,
            dst_ref=dst,
            send_sem=sems[0].at[index],
            recv_sem=sems[1].at[index],
            device_id=peer,
            device_id_type=MESH,
        )
        copy.start()
        return copy

    first = [
        send(part_ref.at[peer], group_buf.at[place], i, {"dp": peer}) for i, peer in enumerate(far)
    ]
    group_buf[place] = part_ref[place]
    for copy in first:
        copy.wait()
    sum_buf[...] = jnp.sum(group_buf[...], axis=0)
    rank_buf[me] = sum_buf[...]
    second = [
        send(sum_buf, rank_buf.at[me], len(first) + i, {"tensor": peer})
        for i, peer in enumerate(others)
    ]
    for copy in second:
        copy.wait()
    out_ref[...] = jnp.sum(rank_buf[...], axis=0)


def farewell(grads):
    groups, ranks = lax.axis_size("dp"), lax.axis_size("tensor")
    kinds, total = grads.shape
    own = total // groups
    wide = -(-own // 128) * 128
    parts = jnp.pad(
        grads.reshape(kinds, groups, own).transpose(1, 0, 2),
        ((0, 0), (0, 8 - kinds), (0, wide - own)),
    )
    whole = pl.BlockSpec(memory_space=pltpu.VMEM)
    summed = pl.pallas_call(
        farewell_kernel,
        name="farewell",
        in_specs=[whole],
        out_specs=whole,
        out_shape=jax.ShapeDtypeStruct((8, wide), jnp.float32),
        scratch_shapes=[
            pltpu.VMEM((groups, 8, wide), jnp.float32),
            pltpu.VMEM((8, wide), jnp.float32),
            pltpu.VMEM((ranks, 8, wide), jnp.float32),
        ]
        + [pltpu.SemaphoreType.DMA((groups + ranks - 2,))] * 2,
        compiler_params=pltpu.CompilerParams(
            collective_id=4, has_side_effects=True, vmem_limit_bytes=4 << 20
        ),
        cost_estimate=pl.CostEstimate(flops=0, bytes_accessed=40 << 20, transcendentals=0),
    )(parts)
    return summed[:kinds, :own]


def stack_kernel(part_ref, whole_ref, own_sem, *sems):
    me, side, cross, diag = tensor_peers()
    step = part_ref.shape[1] // 2
    greet((side, cross))
    own = pltpu.make_async_copy(part_ref, whole_ref.at[me], own_sem)
    own.start()
    cols = [pl.ds(0, step), pl.ds(step, step)]
    over = [
        push(part_ref.at[:, at], whole_ref.at[me, :, at], sems[0:2], i, cross)
        for i, at in enumerate(cols)
    ]
    near = [
        push(part_ref.at[:, at], whole_ref.at[me, :, at], sems[2:4], i, side)
        for i, at in enumerate(cols)
    ]
    relay = []
    for i, at in enumerate(cols):
        over[i].wait_recv()
        relay.append(
            push(whole_ref.at[cross, :, at], whole_ref.at[cross, :, at], sems[4:6], i, side)
        )
    own.wait()
    for i in range(2):
        over[i].wait_send()
        near[i].wait()
        relay[i].wait()


def gather_stack(part):
    return pl.pallas_call(
        stack_kernel,
        name="gather_stack",
        in_specs=[pl.BlockSpec(memory_space=pl.ANY)],
        out_specs=pl.BlockSpec(memory_space=pl.ANY),
        out_shape=jax.ShapeDtypeStruct((4,) + part.shape, part.dtype),
        scratch_shapes=[pltpu.SemaphoreType.DMA] + [pltpu.SemaphoreType.DMA((2,))] * 6,
        compiler_params=pltpu.CompilerParams(
            collective_id=5, has_side_effects=True, vmem_limit_bytes=1 << 20
        ),
        cost_estimate=pl.CostEstimate(flops=0, bytes_accessed=60 << 20, transcendentals=0),
    )(part)


def place_block(piece, start, full_width, axis):
    new_shape = list(piece.shape)
    new_shape[axis] = full_width
    return lax.dynamic_update_slice_in_dim(
        jnp.zeros(tuple(new_shape), jnp.float32), piece, start, axis
    )


BQ = 256
BK = 256


def attn_mask(q_base, k_base, segq_row, segk_col):
    q_pos = q_base + lax.broadcasted_iota(jnp.int32, (BK, BQ), 1)
    k_pos = k_base + lax.broadcasted_iota(jnp.int32, (BK, BQ), 0)
    offset = q_pos - k_pos
    return (offset >= 0) & (offset < WINDOW) & (segk_col == segq_row)


def attn_fwd_kernel(first_ref, qt_ref, k_ref, vt_ref, segr_ref, segc_ref, ot_ref, lse_ref,
                    max_scr, sum_scr, acc_scr):
    heads = qt_ref.shape[0] // HEAD
    block = pl.program_id(1)
    q_base = block * BQ
    max_scr[...] = jnp.full_like(max_scr, MASKED)
    sum_scr[...] = jnp.zeros_like(sum_scr)
    acc_scr[...] = jnp.zeros_like(acc_scr)
    segq_row = segr_ref[0:1, :]

    def body(j, carry):
        k_base = pl.multiple_of(j * BK, BK)
        rows = pl.ds(k_base, BK)
        allowed = attn_mask(q_base, k_base, segq_row, segc_ref[rows, 0:1])
        bias = jnp.where(allowed, 0.0, MASKED)
        k_blk = k_ref[0, rows, :]
        v_blk = vt_ref[:, rows]
        for head in range(heads):
            cols = slice(head * HEAD, (head + 1) * HEAD)
            scores = dot_plain(k_blk, qt_ref[cols, :]) * 0.125 + bias
            old_max = max_scr[head : head + 1]
            new_max = jnp.maximum(old_max, jnp.max(scores, axis=0, keepdims=True))
            expo = jnp.exp(scores - new_max)
            ratio = jnp.exp(old_max - new_max)
            max_scr[head : head + 1] = new_max
            sum_scr[head : head + 1] = sum_scr[head : head + 1] * ratio + jnp.sum(
                expo, axis=0, keepdims=True
            )
            acc_scr[cols] = acc_scr[cols] * ratio + dot_plain(v_blk, expo.astype(jnp.bfloat16))
        return carry

    lax.fori_loop(first_ref[pl.program_id(0) * pl.num_programs(1) + block], block + 1, body, 0)
    for head in range(heads):
        cols = slice(head * HEAD, (head + 1) * HEAD)
        total = jnp.maximum(sum_scr[head : head + 1], 1e-30)
        ot_ref[cols] = (acc_scr[cols] / total).astype(jnp.bfloat16)
        lse_ref[0, head : head + 1] = max_scr[head : head + 1] + jnp.log(total)


def attn_forward(first, q_t, k_rows, v_t, seg_row, seg_col):
    width, tokens = q_t.shape
    slots = k_rows.shape[0]
    group = width // slots
    return pl.pallas_call(
        attn_fwd_kernel,
        name="attn_fwd",
        grid_spec=pltpu.PrefetchScalarGridSpec(
            num_scalar_prefetch=1,
            grid=(slots, tokens // BQ),
            in_specs=[
                pl.BlockSpec((group, BQ), lambda s, i, f: (s, i)),
                pl.BlockSpec((1, tokens, HEAD), lambda s, i, f: (s, 0, 0)),
                pl.BlockSpec((HEAD, tokens), lambda s, i, f: (s, 0)),
                pl.BlockSpec((1, BQ), lambda s, i, f: (0, i)),
                pl.BlockSpec((tokens, 8), lambda s, i, f: (0, 0)),
            ],
            out_specs=[
                pl.BlockSpec((group, BQ), lambda s, i, f: (s, i)),
                pl.BlockSpec((1, 8, BQ), lambda s, i, f: (s, 0, i)),
            ],
            scratch_shapes=[
                pltpu.VMEM((8, BQ), jnp.float32),
                pltpu.VMEM((8, BQ), jnp.float32),
                pltpu.VMEM((group, BQ), jnp.float32),
            ],
        ),
        out_shape=[
            jax.ShapeDtypeStruct((width, tokens), jnp.bfloat16),
            jax.ShapeDtypeStruct((slots, 8, tokens), jnp.float32),
        ],
        compiler_params=pltpu.CompilerParams(vmem_limit_bytes=40 << 20),
        cost_estimate=pl.CostEstimate(
            flops=0, bytes_accessed=198 << 20, transcendentals=0
        ),
    )(first, q_t, k_rows, v_t, seg_row, seg_col)


def attn_bwd_kernel(first_ref, qt_ref, dot_ref, ot_ref, lse_ref, k_ref, kt_ref, v_ref,
                    segr_ref, segc_ref, gqt_ref, gk_ref, gv_ref, delta_scr, acc_scr, q_ref, do_ref):
    heads = qt_ref.shape[0] // HEAD
    block = pl.program_id(1)
    q_base = block * BQ

    @pl.when(block == 0)
    def _():
        gk_ref[...] = jnp.zeros_like(gk_ref)
        gv_ref[...] = jnp.zeros_like(gv_ref)

    acc_scr[...] = jnp.zeros_like(acc_scr)
    for head in range(heads):
        cols = slice(head * HEAD, (head + 1) * HEAD)
        delta_scr[head : head + 1] = jnp.sum(
            dot_ref[cols].astype(jnp.float32) * ot_ref[cols].astype(jnp.float32),
            axis=0,
            keepdims=True,
        )
        q_ref[head] = jnp.transpose(qt_ref[cols].astype(jnp.float32)).astype(jnp.bfloat16)
        do_ref[head] = jnp.transpose(dot_ref[cols].astype(jnp.float32)).astype(jnp.bfloat16)
    segq_row = segr_ref[0:1, :]

    def body(j, carry):
        k_base = pl.multiple_of(j * BK, BK)
        rows = pl.ds(k_base, BK)
        allowed = attn_mask(q_base, k_base, segq_row, segc_ref[rows, 0:1])
        bias = jnp.where(allowed, 0.0, MASKED)
        k_blk = k_ref[0, rows, :]
        kt_blk = kt_ref[:, rows]
        v_blk = v_ref[0, rows, :]
        gk = jnp.zeros((BK, HEAD), jnp.float32)
        gv = jnp.zeros((BK, HEAD), jnp.float32)
        for head in range(heads):
            cols = slice(head * HEAD, (head + 1) * HEAD)
            scores = dot_plain(k_blk, qt_ref[cols, :]) * 0.125 + bias
            probs = jnp.exp(scores - lse_ref[0, head : head + 1])
            grad_p = dot_plain(v_blk, dot_ref[cols, :])
            grad_s = (probs * (grad_p - delta_scr[head : head + 1])).astype(jnp.bfloat16)
            gv += dot_plain(probs.astype(jnp.bfloat16), do_ref[head])
            gk += dot_plain(grad_s, q_ref[head])
            acc_scr[cols] += dot_plain(kt_blk, grad_s)
        gk_ref[0, rows, :] += gk * 0.125
        gv_ref[0, rows, :] += gv
        return carry

    lax.fori_loop(first_ref[pl.program_id(0) * pl.num_programs(1) + block], block + 1, body, 0)
    gqt_ref[...] = (acc_scr[...] * 0.125).astype(jnp.bfloat16)


def attn_backward(first, q_t, do_t, o_t, lse, k_rows, k_t, v_rows, seg_row, seg_col):
    width, tokens = q_t.shape
    slots = k_rows.shape[0]
    group = width // slots
    per = group // HEAD
    tall = pl.BlockSpec((group, BQ), lambda s, i, f: (s, i))
    keyed = pl.BlockSpec((1, tokens, HEAD), lambda s, i, f: (s, 0, 0))
    return pl.pallas_call(
        attn_bwd_kernel,
        name="attn_bwd",
        grid_spec=pltpu.PrefetchScalarGridSpec(
            num_scalar_prefetch=1,
            grid=(slots, tokens // BQ),
            in_specs=[
                tall,
                tall,
                tall,
                pl.BlockSpec((1, 8, BQ), lambda s, i, f: (s, 0, i)),
                keyed,
                pl.BlockSpec((HEAD, tokens), lambda s, i, f: (s, 0)),
                keyed,
                pl.BlockSpec((1, BQ), lambda s, i, f: (0, i)),
                pl.BlockSpec((tokens, 8), lambda s, i, f: (0, 0)),
            ],
            out_specs=[tall, keyed, keyed],
            scratch_shapes=[
                pltpu.VMEM((8, BQ), jnp.float32),
                pltpu.VMEM((group, BQ), jnp.float32),
                pltpu.VMEM((per, BQ, HEAD), jnp.bfloat16),
                pltpu.VMEM((per, BQ, HEAD), jnp.bfloat16),
            ],
        ),
        out_shape=[
            jax.ShapeDtypeStruct((width, tokens), jnp.bfloat16),
            jax.ShapeDtypeStruct((slots, tokens, HEAD), jnp.float32),
            jax.ShapeDtypeStruct((slots, tokens, HEAD), jnp.float32),
        ],
        compiler_params=pltpu.CompilerParams(vmem_limit_bytes=40 << 20),
        cost_estimate=pl.CostEstimate(
            flops=0, bytes_accessed=190 << 20, transcendentals=0
        ),
    )(first, q_t, do_t, o_t, lse, k_rows, k_t, v_rows, seg_row, seg_col)


def first_blocks(segs_flat):
    tokens = segs_flat.shape[0]
    starts = segs_flat[::BQ]
    positions = jnp.arange(tokens // BQ, dtype=jnp.int32) * BQ
    seg_start = jnp.sum((segs_flat[None, :] < starts[:, None]).astype(jnp.int32), axis=1)
    return jnp.maximum(jnp.maximum(seg_start, positions - WINDOW + 1), 0) // BK


def conv_rows(x_in, conv_w, conv_b, segs_grid):
    seq_count, seq_len = segs_grid.shape
    width = x_in.shape[1]
    grid = x_in.reshape(seq_count, seq_len, width)
    pad_x = jnp.concatenate([jnp.zeros((seq_count, CONV - 1, width), jnp.float32), grid], axis=1)
    pad_seg = jnp.concatenate([jnp.full((seq_count, CONV - 1), -1, jnp.int32), segs_grid], axis=1)
    total = jnp.zeros((seq_count, seq_len, width), jnp.float32) + conv_b
    for tap in range(CONV):
        same = (pad_seg[:, tap : tap + seq_len] == segs_grid).astype(jnp.float32)
        total = total + conv_w[tap] * pad_x[:, tap : tap + seq_len] * same[:, :, None]
    return jax.nn.silu(total).reshape(seq_count * seq_len, width)


CHUNK = 64
ROWS = 256
RANGE = 100.0
LANES = 256


def spans(width, size):
    return [(at, min(at + size, width)) for at in range(0, width, size)]


def softplus_parts(pre):
    small = jnp.exp(-jnp.abs(pre))
    step = jnp.maximum(pre, 0.0) + jnp.log1p(small)
    slope = jnp.where(pre >= 0.0, 1.0, small) / (1.0 + small)
    return step, slope


def split_sum(tri, values):
    high = values.astype(jnp.bfloat16)
    low = (values - high.astype(jnp.float32)).astype(jnp.bfloat16)
    return dot_plain(tri, high) + dot_plain(tri, low)


def tri_matrix(upper):
    row = lax.broadcasted_iota(jnp.int32, (CHUNK, CHUNK), 0)
    col = lax.broadcasted_iota(jnp.int32, (CHUNK, CHUNK), 1)
    return (col >= row) if upper else (row >= col)


def scan_setup(dbl_ref, dtw_ref, vec_ref, xa_ref, step_scr, cum_scr, slope_scr):
    width = xa_ref.shape[1]
    tri = tri_matrix(False).astype(jnp.bfloat16)
    lowest = jnp.zeros((), jnp.float32)
    for lo, hi in spans(width, LANES):
        bias = vec_ref[0:1, lo:hi]
        rate = jnp.exp(vec_ref[1:2, lo:hi])
        least = jnp.zeros((1, hi - lo), jnp.float32)
        for at in range(0, ROWS, CHUNK):
            pre = dot_plain(dbl_ref[at : at + CHUNK, :RANK], dtw_ref[:, lo:hi]) + bias
            step, slope = softplus_parts(pre)
            cum = split_sum(tri, -step * rate)
            step_scr[at : at + CHUNK, lo:hi] = step
            cum_scr[at : at + CHUNK, lo:hi] = cum
            if slope_scr is not None:
                slope_scr[at : at + CHUNK, lo:hi] = slope
            least = jnp.minimum(least, cum[CHUNK - 1 : CHUNK])
        lowest = jnp.minimum(lowest, jnp.min(least))
    return lowest


def chunk_maps(dbl_ref, mask_ref, segr_ref, at):
    rows = slice(at, at + CHUNK)
    b_map = dbl_ref[rows, 128 : 128 + STATE]
    c_map = dbl_ref[rows, 128 + STATE : 128 + 2 * STATE]
    linked = mask_ref[rows, 0:1]
    tail = mask_ref[rows, 1:2]
    keep = mask_ref[at + CHUNK - 1 : at + CHUNK, 2:3]
    allowed = tri_matrix(False) & (mask_ref[rows, 4:5] == segr_ref[0:1, rows])
    gram = jnp.where(allowed, dot_last(c_map, b_map), 0.0).astype(jnp.bfloat16)
    c_link = (c_map.astype(jnp.float32) * linked).astype(jnp.bfloat16)
    b_tail = (b_map.astype(jnp.float32) * tail).astype(jnp.bfloat16)
    return b_map, c_map, linked, tail, keep, allowed, gram, c_link, b_tail


def token_column(block, lane_index):
    lanes = lax.broadcasted_iota(jnp.int32, block.shape, 1)
    return jnp.sum(jnp.where(lanes == lane_index, block, 0.0), axis=1, keepdims=True)


def scan_fwd_kernel(
    xa_ref, z_ref, dbl_ref, mask_ref, segr_ref, dtw_ref, vec_ref,
    out_ref, hsave_ref, h_scr, step_scr, cum_scr, y_scr,
):
    width = xa_ref.shape[1]

    @pl.when(pl.program_id(0) == 0)
    def _():
        h_scr[...] = jnp.zeros_like(h_scr)

    lowest = scan_setup(dbl_ref, dtw_ref, vec_ref, xa_ref, step_scr, cum_scr, None)

    @pl.when(lowest >= -RANGE)
    def _():
        for index, at in enumerate(range(0, ROWS, CHUNK)):
            rows = slice(at, at + CHUNK)
            _, _, _, _, keep, _, gram, c_link, b_tail = chunk_maps(dbl_ref, mask_ref, segr_ref, at)
            for lo, hi in spans(width, LANES):
                cum = cum_scr[rows, lo:hi]
                half = 0.5 * cum[CHUNK - 1 : CHUNK]
                gap = cum - half
                rise = jnp.exp(half)
                h_old = h_scr[:, lo:hi]
                hsave_ref[index, :, lo:hi] = h_old
                x_f = xa_ref[rows, lo:hi].astype(jnp.float32)
                drive = (jnp.exp(-gap) * (step_scr[rows, lo:hi] * x_f)).astype(jnp.bfloat16)
                inner = dot_plain(gram, drive) + dot_plain(
                    c_link, (rise * h_old).astype(jnp.bfloat16)
                )
                total = jnp.exp(gap) * inner + vec_ref[2:3, lo:hi] * x_f
                out_ref[rows, lo:hi] = (total * jax.nn.silu(z_ref[rows, lo:hi])).astype(
                    jnp.bfloat16
                )
                h_scr[:, lo:hi] = rise * dot_first(b_tail, drive) + (rise * rise * keep) * h_old

    @pl.when(lowest < -RANGE)
    def _():
        for index, at in enumerate(range(0, ROWS, CHUNK)):
            rows = slice(at, at + CHUNK)
            hsave_ref[index] = h_scr[...]
            b_cols = jnp.transpose(dbl_ref[rows, 128 : 128 + STATE].astype(jnp.float32))
            c_cols = jnp.transpose(dbl_ref[rows, 128 + STATE : 128 + 2 * STATE].astype(jnp.float32))
            y_scr[...] = xa_ref[rows].astype(jnp.float32)
            rate = jnp.exp(vec_ref[1:2])

            def token(t, carry):
                step = step_scr[pl.ds(at + t, 1)]
                keep = mask_ref[pl.ds(at + t, 1)][:, 3:4]
                state = (jnp.exp(-step * rate) * keep) * h_scr[...] + token_column(b_cols, t) * (
                    step * y_scr[pl.ds(t, 1)]
                )
                h_scr[...] = state
                y_scr[pl.ds(t, 1)] = (
                    jnp.sum(state * token_column(c_cols, t), axis=0, keepdims=True)
                    + vec_ref[2:3] * y_scr[pl.ds(t, 1)]
                )
                return carry

            lax.fori_loop(0, CHUNK, token, 0)
            out_ref[rows] = (y_scr[...] * jax.nn.silu(z_ref[rows])).astype(jnp.bfloat16)


def scan_bwd_kernel(
    xa_ref, z_ref, dbl_ref, mask_ref, segr_ref, dtw_ref, vec_ref, hsave_ref, gs_ref,
    gz_ref, gx_ref, gdbl_ref, gdtw_ref, gvec_ref,
    g_scr, step_scr, cum_scr, slope_scr, gl_scr, gu_scr, hall_scr, y_scr,
):
    width = xa_ref.shape[1]

    @pl.when(pl.program_id(0) == 0)
    def _():
        g_scr[...] = jnp.zeros_like(g_scr)
        gdtw_ref[...] = jnp.zeros_like(gdtw_ref)
        gvec_ref[...] = jnp.zeros_like(gvec_ref)

    lowest = scan_setup(dbl_ref, dtw_ref, vec_ref, xa_ref, step_scr, cum_scr, slope_scr)
    triu = tri_matrix(True).astype(jnp.bfloat16)
    count = ROWS // CHUNK

    def finish(at, lo, hi, gu, gl, gy, first):
        rows = slice(at, at + CHUNK)
        step = step_scr[rows, lo:hi]
        x_f = xa_ref[rows, lo:hi].astype(jnp.float32)
        rate = jnp.exp(vec_ref[1:2, lo:hi])
        gx_ref[rows, lo:hi] = step * gu + vec_ref[2:3, lo:hi] * gy
        gpre = (x_f * gu - rate * gl) * slope_scr[rows, lo:hi]
        gvec_ref[0:1, lo:hi] += jnp.sum(gpre, axis=0, keepdims=True)
        gvec_ref[1:2, lo:hi] += jnp.sum(-step * rate * gl, axis=0, keepdims=True)
        gvec_ref[2:3, lo:hi] += jnp.sum(gy * x_f, axis=0, keepdims=True)
        gpre_low = gpre.astype(jnp.bfloat16)
        gdtw_ref[:, lo:hi] += dot_first(dbl_ref[rows, :RANK], gpre_low)
        part = dot_last(gpre_low, dtw_ref[:, lo:hi])
        if first:
            gdbl_ref[rows, :RANK] = part
        else:
            gdbl_ref[rows, :RANK] += part

    def gate_grads(rows, lo, hi, total):
        z_f = z_ref[rows, lo:hi]
        grad = gs_ref[rows, lo:hi]
        sig = jax.nn.sigmoid(z_f)
        gz_ref[rows, lo:hi] = (grad * total * (sig * (1.0 + z_f * (1.0 - sig)))).astype(
            jnp.bfloat16
        )

    def gate_pull(rows, lo, hi):
        return gs_ref[rows, lo:hi] * jax.nn.silu(z_ref[rows, lo:hi])

    @pl.when(lowest >= -RANGE)
    def _():
        for index in range(count - 1, -1, -1):
            at = index * CHUNK
            rows = slice(at, at + CHUNK)
            b_map, c_map, linked, tail, keep, allowed, gram, c_link, b_tail = chunk_maps(
                dbl_ref, mask_ref, segr_ref, at
            )
            g_gram = jnp.zeros((CHUNK, CHUNK), jnp.float32)
            g_c = jnp.zeros((CHUNK, STATE), jnp.float32)
            g_b = jnp.zeros((CHUNK, STATE), jnp.float32)
            for lo, hi in spans(width, LANES):
                cum = cum_scr[rows, lo:hi]
                half = 0.5 * cum[CHUNK - 1 : CHUNK]
                gap = cum - half
                fall = jnp.exp(gap)
                grow = jnp.exp(-gap)
                rise = jnp.exp(half)
                h_old = hsave_ref[index, :, lo:hi]
                g_new = g_scr[:, lo:hi]
                x_f = xa_ref[rows, lo:hi].astype(jnp.float32)
                drive = (grow * (step_scr[rows, lo:hi] * x_f)).astype(jnp.bfloat16)
                h_low = (rise * h_old).astype(jnp.bfloat16)
                g_low = (rise * g_new).astype(jnp.bfloat16)
                inner = dot_plain(gram, drive) + dot_plain(c_link, h_low)
                gate_grads(rows, lo, hi, fall * inner + vec_ref[2:3, lo:hi] * x_f)
                gy = gate_pull(rows, lo, hi)
                pulled = (fall * gy).astype(jnp.bfloat16)
                back = dot_first(gram, pulled) + dot_plain(b_tail, g_low)
                g_gram += dot_last(pulled, drive)
                g_c += dot_last(pulled, h_low)
                g_b += dot_last(drive, g_low)
                pushed = dot_first(b_tail, drive)
                ends = jnp.sum(g_low.astype(jnp.float32) * pushed, axis=0, keepdims=True) + (
                    rise * rise * keep
                ) * jnp.sum(g_new * h_old, axis=0, keepdims=True)
                diff = (
                    pulled.astype(jnp.float32) * inner - drive.astype(jnp.float32) * back
                )
                gl = split_sum(triu, diff) + ends
                g_scr[:, lo:hi] = rise * dot_first(c_link, pulled) + (rise * rise * keep) * g_new
                finish(at, lo, hi, grow * back, gl, gy, lo == 0)
            g_gram = jnp.where(allowed, g_gram, 0.0).astype(jnp.bfloat16)
            gdbl_ref[rows, 128 : 128 + STATE] = dot_first(g_gram, c_map) + tail * g_b
            gdbl_ref[rows, 128 + STATE : 128 + 2 * STATE] = dot_plain(g_gram, b_map) + linked * g_c

    @pl.when(lowest < -RANGE)
    def _():
        rate = jnp.exp(vec_ref[1:2])

        def chunk_step(reverse, carry):
            index = count - 1 - reverse
            at = pl.multiple_of(index * CHUNK, CHUNK)
            rows = pl.ds(at, CHUNK)
            b_cols = jnp.transpose(dbl_ref[rows, 128 : 128 + STATE].astype(jnp.float32))
            c_cols = jnp.transpose(dbl_ref[rows, 128 + STATE : 128 + 2 * STATE].astype(jnp.float32))
            hall_scr[0] = hsave_ref[index]
            y_scr[...] = xa_ref[rows].astype(jnp.float32)
            gu_scr[...] = gate_pull(rows, 0, width)

            def forward(t, inner_carry):
                step = step_scr[pl.ds(at + t, 1)]
                keep = mask_ref[pl.ds(at + t, 1)][:, 3:4]
                state = (jnp.exp(-step * rate) * keep) * hall_scr[t] + token_column(b_cols, t) * (
                    step * y_scr[pl.ds(t, 1)]
                )
                hall_scr[t + 1] = state
                return inner_carry

            lax.fori_loop(0, CHUNK, forward, 0)

            def backward(back, inner_carry):
                g_b, g_c = inner_carry
                t = CHUNK - 1 - back
                step = step_scr[pl.ds(at + t, 1)]
                keep = mask_ref[pl.ds(at + t, 1)][:, 3:4]
                decay = jnp.exp(-step * rate) * keep
                gy = gu_scr[pl.ds(t, 1)]
                x_f = y_scr[pl.ds(t, 1)]
                c_col = token_column(c_cols, t)
                b_col = token_column(b_cols, t)
                here = hall_scr[t + 1]
                grad = g_scr[...] + c_col * gy
                lanes = lax.broadcasted_iota(jnp.int32, (STATE, CHUNK), 1)
                g_b = jnp.where(
                    lanes == t, jnp.sum(grad * (step * x_f), axis=1, keepdims=True), g_b
                )
                g_c = jnp.where(lanes == t, jnp.sum(here * gy, axis=1, keepdims=True), g_c)
                gl_scr[pl.ds(t, 1)] = decay * jnp.sum(grad * hall_scr[t], axis=0, keepdims=True)
                gu_scr[pl.ds(t, 1)] = jnp.sum(grad * b_col, axis=0, keepdims=True)
                y_scr[pl.ds(t, 1)] = (
                    jnp.sum(here * c_col, axis=0, keepdims=True) + vec_ref[2:3] * x_f
                )
                g_scr[...] = decay * grad
                return g_b, g_c

            blank = jnp.zeros((STATE, CHUNK), jnp.float32)
            g_b, g_c = lax.fori_loop(0, CHUNK, backward, (blank, blank))
            gdbl_ref[rows, 128 : 128 + STATE] = jnp.transpose(g_b)
            gdbl_ref[rows, 128 + STATE : 128 + 2 * STATE] = jnp.transpose(g_c)
            z_f = z_ref[rows]
            grad = gs_ref[rows]
            sig = jax.nn.sigmoid(z_f)
            gz_ref[rows] = (grad * y_scr[...] * (sig * (1.0 + z_f * (1.0 - sig)))).astype(
                jnp.bfloat16
            )
            gy = grad * (z_f * sig)
            step = step_scr[rows]
            x_f = xa_ref[rows].astype(jnp.float32)
            gu, gl = gu_scr[...], gl_scr[...]
            gx_ref[rows] = step * gu + vec_ref[2:3] * gy
            gpre = (x_f * gu - rate * gl) * slope_scr[rows]
            gvec_ref[0:1] += jnp.sum(gpre, axis=0, keepdims=True)
            gvec_ref[1:2] += jnp.sum(-step * rate * gl, axis=0, keepdims=True)
            gvec_ref[2:3] += jnp.sum(gy * x_f, axis=0, keepdims=True)
            gpre_low = gpre.astype(jnp.bfloat16)
            gdtw_ref[...] += dot_first(dbl_ref[rows, :RANK], gpre_low)
            gdbl_ref[rows, :RANK] = dot_last(gpre_low, dtw_ref[...])
            return carry

        lax.fori_loop(0, count, chunk_step, 0)


def scan_specs(width, backward, blocks):
    def at(i):
        return (blocks - 1 - i) if backward else i

    rows = lambda cols: pl.BlockSpec((ROWS, cols), lambda i: (at(i), 0))
    whole = lambda *shape: pl.BlockSpec(shape, lambda i: (0, 0))
    return [
        rows(width),
        rows(width),
        rows(256),
        rows(8),
        pl.BlockSpec((1, ROWS), lambda i: (0, at(i))),
        whole(RANK, width),
        whole(8, width),
    ], pl.BlockSpec((ROWS // CHUNK, STATE, width), lambda i: (at(i), 0, 0)), rows, whole


def scan_forward(x_act, z_gate, dbl, masks, seg_row, dt_weight, vectors):
    tokens, width = x_act.shape
    blocks = tokens // ROWS
    in_specs, state_spec, rows, whole = scan_specs(width, False, blocks)
    return pl.pallas_call(
        scan_fwd_kernel,
        name="scan_fwd",
        grid=(blocks,),
        in_specs=in_specs,
        out_specs=[rows(width), state_spec],
        out_shape=[
            jax.ShapeDtypeStruct((tokens, width), jnp.bfloat16),
            jax.ShapeDtypeStruct((tokens // CHUNK, STATE, width), jnp.float32),
        ],
        scratch_shapes=[
            pltpu.VMEM((STATE, width), jnp.float32),
            pltpu.VMEM((ROWS, width), jnp.float32),
            pltpu.VMEM((ROWS, width), jnp.float32),
            pltpu.VMEM((CHUNK, width), jnp.float32),
        ],
        compiler_params=pltpu.CompilerParams(vmem_limit_bytes=40 << 20),
        cost_estimate=pl.CostEstimate(
            flops=0, bytes_accessed=93 << 20, transcendentals=0
        ),
    )(x_act, z_gate, dbl, masks, seg_row, dt_weight, vectors)


def scan_backward(x_act, z_gate, dbl, masks, seg_row, dt_weight, vectors, states, grad_rows):
    tokens, width = x_act.shape
    blocks = tokens // ROWS
    in_specs, state_spec, rows, whole = scan_specs(width, True, blocks)
    return pl.pallas_call(
        scan_bwd_kernel,
        name="scan_bwd",
        grid=(blocks,),
        in_specs=in_specs + [state_spec, rows(width)],
        out_specs=[rows(width), rows(width), rows(256), whole(RANK, width), whole(8, width)],
        out_shape=[
            jax.ShapeDtypeStruct((tokens, width), jnp.bfloat16),
            jax.ShapeDtypeStruct((tokens, width), jnp.float32),
            jax.ShapeDtypeStruct((tokens, 256), jnp.float32),
            jax.ShapeDtypeStruct((RANK, width), jnp.float32),
            jax.ShapeDtypeStruct((8, width), jnp.float32),
        ],
        scratch_shapes=[
            pltpu.VMEM((STATE, width), jnp.float32),
            pltpu.VMEM((ROWS, width), jnp.float32),
            pltpu.VMEM((ROWS, width), jnp.float32),
            pltpu.VMEM((ROWS, width), jnp.float32),
            pltpu.VMEM((CHUNK, width), jnp.float32),
            pltpu.VMEM((CHUNK, width), jnp.float32),
            pltpu.VMEM((CHUNK + 1, STATE, width), jnp.float32),
            pltpu.VMEM((CHUNK, width), jnp.float32),
        ],
        compiler_params=pltpu.CompilerParams(vmem_limit_bytes=48 << 20),
        cost_estimate=pl.CostEstimate(
            flops=0, bytes_accessed=244 << 20, transcendentals=0
        ),
    )(x_act, z_gate, dbl, masks, seg_row, dt_weight, vectors, states, grad_rows)


def scan_masks(segs_flat):
    tokens = segs_flat.shape[0]
    before = jnp.concatenate([jnp.full((1,), -1, jnp.int32), segs_flat[:-1]])
    chunked = segs_flat.reshape(tokens // CHUNK, CHUNK)
    prior = before.reshape(tokens // CHUNK, CHUNK)[:, :1]
    last = chunked[:, CHUNK - 1 :]
    linked = chunked == prior
    tail = chunked == last
    keep = jnp.broadcast_to(last == prior, chunked.shape)
    same = (segs_flat == before).reshape(chunked.shape)
    blank = jnp.zeros_like(linked)
    stacked = jnp.stack([linked, tail, keep, same], axis=-1).reshape(tokens, 4).astype(jnp.float32)
    number = segs_flat.astype(jnp.float32)
    masks = jnp.concatenate(
        [stacked, number[:, None], jnp.zeros((tokens, 3), jnp.float32)], axis=1
    )
    return masks, number[None, :]


def per_device(
    inputs,
    teacher,
    segment_ids,
    valid,
    norm_in_gain,
    w_query,
    w_key,
    w_value,
    w_attn_out,
    w_mamba_in,
    conv_weight,
    conv_bias,
    x_proj,
    dt_proj,
    dt_bias,
    a_log,
    d_skip,
    w_mamba_out,
    attn_norm_gain,
    ssm_norm_gain,
    norm_mid_gain,
    w_gate,
    w_up,
    w_down,
):
    rank_index = lax.axis_index("tensor")
    first_slot = jnp.where(rank_index == 0, 0, rank_index + 1)
    second_slot = jnp.where(rank_index == 0, 1, rank_index + 1)
    per_slot = HEADS // KV
    group_width = per_slot * HEAD
    query_width = 2 * group_width
    qkv_width = query_width + 4 * HEAD
    width = inputs.shape[1]
    inner_width = w_mamba_out.shape[0]
    inner_start = rank_index * inner_width
    inner_all = inner_width * lax.axis_size("tensor")
    low = lambda values: values.astype(jnp.bfloat16)
    gather_dp = lambda part: lax.all_gather(part, "dp", axis=0, tiled=True)
    scatter_dp = lambda part: lax.psum_scatter(part, "dp", scatter_dimension=0, tiled=True)
    gather_t = lambda part: gather_rows(part, 1)
    reduce_t = lambda part: reduce_rows(part, 2)
    tie = lax.optimization_barrier

    own_width = w_query.shape[0]
    qkv_local = jnp.concatenate(
        [
            pick_groups(w_query, first_slot, second_slot, group_width, 1),
            pick_groups(w_key, first_slot, second_slot, HEAD, 1),
            pick_groups(w_value, first_slot, second_slot, HEAD, 1),
        ],
        axis=1,
    )
    qkv_w = gather_dp(qkv_local)
    gain_rows = jnp.stack([norm_in_gain, attn_norm_gain, ssm_norm_gain, norm_mid_gain])
    gain_rows, _ = tie((gain_rows, qkv_local))
    gains, valid_total = hello(gain_rows, jnp.sum(valid).astype(jnp.float32))
    gain_in, gain_attn, gain_ssm, gain_mid = [gains[index][:, None] for index in range(4)]
    inputs_t = inputs.T
    normed_in, pull_in = jax.vjp(normalize_t, inputs_t, gain_in)
    normed_low, x_proj, dt_proj, conv_weight, w_mamba_in = tie(
        (low(normed_in), x_proj, dt_proj, conv_weight, w_mamba_in)
    )
    inner_local = jnp.concatenate(
        [
            dt_bias[:, None],
            a_log[:, None],
            d_skip[:, None],
            conv_bias[:, None],
            conv_weight.T,
            x_proj,
            dt_proj.T,
        ],
        axis=1,
    ).reshape(own_width, -1)
    mamba_local = jnp.concatenate(
        [
            w_mamba_in.reshape(own_width, 2 * inner_width),
            jnp.zeros((own_width, -2 * inner_width % 128), jnp.bfloat16),
            inner_local,
        ],
        axis=1,
    )
    mamba_all = gather_dp(mamba_local)
    normed_low, _ = tie((normed_low, mamba_local))
    whole_in = gather_t(normed_low)
    whole_in, w_attn_out, w_mamba_out, w_gate, w_up, w_down = tie(
        (whole_in, w_attn_out, w_mamba_out, w_gate, w_up, w_down)
    )
    out_local = jnp.concatenate(
        [pick_groups(w_attn_out, first_slot, second_slot, group_width, 0).T, w_mamba_out.T], axis=1
    )
    outs_all = gather_dp(out_local)
    ff_width = w_gate.shape[1]
    ff_step = -(-ff_width // 128) * 128
    blank = jnp.zeros((own_width, ff_step - ff_width), jnp.bfloat16)
    qkv_cols = low(dot_first(qkv_w, whole_in))
    qkv_cols, w_gate, w_up, w_down = tie((qkv_cols, w_gate, w_up, w_down))
    gate_up_all = gather_dp(jnp.concatenate([w_gate, blank, w_up, blank], axis=1))
    queries_t = qkv_cols[:query_width]
    keys_t = qkv_cols[query_width : query_width + 2 * HEAD]
    values_t = qkv_cols[query_width + 2 * HEAD :]
    group_rows = whole_in.shape[1]
    seq_count = group_rows // LEN
    segs_grid = segment_ids.reshape(seq_count, LEN)
    segs_flat = (segs_grid + 128 * jnp.arange(seq_count, dtype=jnp.int32)[:, None]).reshape(-1)
    scan_mask, seg_row = scan_masks(segs_flat)
    seg_col = jnp.broadcast_to(segs_flat.astype(jnp.float32)[:, None], (group_rows, 8))
    starts = first_blocks(segs_flat)
    blocks = jnp.arange(group_rows // BQ, dtype=jnp.int32)
    firsts = jnp.concatenate([starts, jnp.where(rank_index == 0, starts, blocks + 1)])
    keys_r = keys_t.reshape(2, HEAD, group_rows).transpose(0, 2, 1)
    values_r = values_t.reshape(2, HEAD, group_rows).transpose(0, 2, 1)
    attended_t, log_totals = attn_forward(firsts, queries_t, keys_r, values_t, seg_row, seg_col)
    attended_t, mamba_all, w_down = tie((attended_t, mamba_all, w_down))
    down_all = gather_dp(w_down.T)
    inner_rows = lax.dynamic_slice_in_dim(
        mamba_all[:, -inner_local.shape[1] :].reshape(inner_all, -1), inner_start, inner_width, 0
    )

    vector_rows = inner_rows[:, :8].astype(jnp.float32).T
    xproj_rows = inner_rows[:, 8 : 8 + RANK + 2 * STATE]
    dt_weight = inner_rows[:, 8 + RANK + 2 * STATE :].T
    xproj_pad = jnp.concatenate(
        [
            xproj_rows[:, :RANK],
            jnp.zeros((inner_width, 128 - RANK), jnp.bfloat16),
            xproj_rows[:, RANK:],
            jnp.zeros((inner_width, 128 - 2 * STATE), jnp.bfloat16),
        ],
        axis=1,
    )
    weight_x = mamba_all[:, :inner_width]
    weight_z = mamba_all[:, inner_width : 2 * inner_width]
    x_in = dot_first(whole_in, weight_x)
    x_pre, pull_conv = jax.vjp(
        lambda x_part, taps, shift: conv_rows(x_part, taps, shift, segs_grid),
        x_in,
        vector_rows[4:],
        vector_rows[3],
    )
    x_act = low(x_pre)
    dbl_pad = total_rows(dot_plain(x_act, xproj_pad), 3)
    z_gate = dot_first(whole_in, weight_z)
    ssm_rows, states = scan_forward(
        x_act, z_gate, dbl_pad, scan_mask, seg_row, dt_weight, vector_rows
    )
    attended_t, ssm_rows, outs_all = tie((attended_t, ssm_rows, outs_all))
    out_w = outs_all[:, :query_width]
    mamba_out_w = outs_all[:, query_width:]
    attn_sum = reduce_t(low(dot_plain(out_w, attended_t)))
    ssm_part = low(dot_last(mamba_out_w, ssm_rows))
    ssm_part, attn_sum = tie((ssm_part, attn_sum))
    ssm_sum = reduce_t(ssm_part)
    mixed, pull_join = jax.vjp(join_rows_t, inputs_t, attn_sum, ssm_sum, gain_attn, gain_ssm)
    normed_mid, pull_mid = jax.vjp(normalize_t, mixed, gain_mid)
    whole_mid = gather_t(low(normed_mid))
    whole_mid, gate_up_all = tie((whole_mid, gate_up_all))
    gate_all = gate_up_all[:, :ff_width]
    up_all = gate_up_all[:, ff_step : ff_step + ff_width]
    gate_rows = dot_first(whole_mid, gate_all)
    up_rows = dot_first(whole_mid, up_all)
    sigmoid_gate = jax.nn.sigmoid(gate_rows)
    hidden = low(gate_rows * sigmoid_gate * up_rows)
    ffn_rows = reduce_t(low(dot_last(down_all, hidden)))
    result = mixed + ffn_rows
    all_rows = inputs.shape[0] * lax.axis_size("dp") * lax.axis_size("tensor")
    grad_out = all_rows / valid_total * valid.astype(jnp.float32)[None, :] * (result - teacher.T)
    grad_ffn = gather_t(low(grad_out))
    grad_hidden = dot_first(grad_ffn, down_all)
    grad_gate = low(grad_hidden * up_rows * sigmoid_gate * (1.0 + gate_rows * (1.0 - sigmoid_gate)))
    grad_up = low(grad_hidden * gate_rows * sigmoid_gate)
    ffn_grads = weight_grads(
        [
            (whole_mid, grad_gate, False),
            (whole_mid, grad_up, False),
            (grad_ffn, hidden, False),
        ],
        "ffn_weight_grads",
        44,
    )
    grad_gate, grad_up, ffn_grads = tie((grad_gate, grad_up, ffn_grads))
    ffn_shard = scatter_dp(ffn_grads)
    mid_part = low(dot_last(gate_all, grad_gate) + dot_last(up_all, grad_up))
    grad_mid_rows = reduce_t(mid_part)
    grad_mixed_norm, grad_gain_mid = pull_mid(grad_mid_rows)
    grad_mixed = grad_out + grad_mixed_norm
    grad_resid, grad_attn_sum, grad_ssm_sum, grad_gain_attn, grad_gain_ssm = pull_join(grad_mixed)
    grad_ssm_whole = gather_t(low(grad_ssm_sum))
    grad_attn_low, grad_ssm_whole = tie((low(grad_attn_sum), grad_ssm_whole))
    grad_attn_whole = gather_t(grad_attn_low)
    grad_ssm_whole, grad_attn_whole = tie((grad_ssm_whole, grad_attn_whole))
    grad_ssm_rows = dot_first(grad_ssm_whole, mamba_out_w)
    grad_gate_part, grad_act_scan, grad_dbl_part, grad_dtproj, grad_vectors = scan_backward(
        x_act, z_gate, dbl_pad, scan_mask, seg_row, dt_weight, vector_rows, states, grad_ssm_rows
    )
    mid_grads = weight_grads(
        [
            (grad_attn_whole, attended_t, True),
            (grad_ssm_whole, ssm_rows, False),
            (whole_in, grad_gate_part, False),
        ],
        "mid_weight_grads",
        26,
        128,
    )
    grad_att_t = low(
        lax.dot_general(
            out_w, grad_attn_whole, (((0,), (0,)), ((), ())), preferred_element_type=jnp.float32
        )
    )
    grad_dbl_part, mid_grads, ffn_shard = tie((grad_dbl_part, mid_grads, ffn_shard))
    mid_shard = scatter_dp(mid_grads)
    grad_queries_t, grad_keys, grad_values = attn_backward(
        firsts,
        queries_t,
        grad_att_t,
        attended_t,
        log_totals,
        keys_r,
        keys_t,
        values_r,
        seg_row,
        seg_col,
    )
    columns_of = lambda rows: low(rows.transpose(0, 2, 1).reshape(2 * HEAD, group_rows))
    grad_qkv = jnp.concatenate(
        [grad_queries_t, columns_of(grad_keys), columns_of(grad_values)], axis=0
    )
    grad_dbl = total_rows(grad_dbl_part, 3)
    grad_act = grad_act_scan + dot_last(grad_dbl, xproj_pad)
    grad_xproj_w = dot_first(x_act, grad_dbl)
    grad_x_part, grad_taps, grad_shift = pull_conv(grad_act)
    grad_x_low = low(grad_x_part)
    inner_grads = jnp.concatenate(
        [
            grad_vectors[:3].T,
            grad_shift[:, None],
            grad_taps.T,
            grad_xproj_w[:, :RANK],
            grad_xproj_w[:, 128 : 128 + 2 * STATE],
            grad_dtproj.T,
        ],
        axis=1,
    )
    inner_full = low(place_block(inner_grads, inner_start, inner_all, 0)).reshape(width, -1)
    last_grads = weight_grads(
        [(whole_in, grad_x_low, False), (whole_in, grad_qkv, True), (inner_full, None, False)],
        "last_weight_grads",
        20,
    )
    grad_x_low, grad_qkv, last_grads, mid_shard = tie(
        (grad_x_low, grad_qkv, last_grads, mid_shard)
    )
    last_shard = scatter_dp(last_grads)
    in_part = low(
        dot_plain(qkv_w, grad_qkv)
        + dot_last(weight_x, grad_x_low)
        + dot_last(weight_z, grad_gate_part)
    )
    grad_in_rows = reduce_t(in_part)
    grad_in_norm, grad_gain_in = pull_in(grad_in_rows)
    grad_inputs = grad_resid + grad_in_norm
    gain_grads = jnp.concatenate(
        [grad_gain_in, grad_gain_attn, grad_gain_ssm, grad_gain_mid], axis=1
    )
    gains_own = farewell(gain_grads.T)
    gains_own, last_shard, grad_inputs = tie((gains_own, last_shard, grad_inputs))
    inner_step = -(-inner_width // 128) * 128
    shared = jnp.concatenate(
        [
            last_shard[:, inner_step : inner_step + qkv_width],
            mid_shard[:, :query_width],
            last_shard[:, inner_step + qkv_width : inner_step + qkv_width + inner_full.shape[1]],
        ],
        axis=1,
    )
    shared = jnp.pad(shared, ((0, 0), (0, -shared.shape[1] % 256)))
    shared_all = gather_stack(shared)
    inner_sum = jnp.sum(
        shared_all[:, :, qkv_width + query_width : qkv_width + query_width + inner_full.shape[1]].astype(jnp.float32), axis=0
    ).reshape(inner_all // lax.axis_size("dp"), -1)
    mamba_at = query_width
    gate_at = query_width + inner_step
    ranks = [0] + list(range(lax.axis_size("tensor")))
    slots = [0, 1] + [0] * (lax.axis_size("tensor") - 1)

    def merge(start, size):
        parts = [
            shared_all[rank, :, start + slot * size : start + (slot + 1) * size]
            for rank, slot in zip(ranks, slots)
        ]
        return jnp.concatenate(parts, axis=1).astype(jnp.float32)

    return (
        result.T,
        grad_inputs.T,
        gains_own[0],
        merge(0, group_width),
        merge(query_width, HEAD),
        merge(query_width + 2 * HEAD, HEAD),
        merge(qkv_width, group_width).T,
        jnp.stack(
            [last_shard[:, :inner_width], mid_shard[:, gate_at : gate_at + inner_width]], axis=1
        ).astype(jnp.float32),
        inner_sum[:, 4:8].T,
        inner_sum[:, 3],
        inner_sum[:, 8 : 8 + RANK + 2 * STATE],
        inner_sum[:, 8 + RANK + 2 * STATE :].T,
        inner_sum[:, 0],
        inner_sum[:, 1],
        inner_sum[:, 2],
        mid_shard[:, mamba_at : mamba_at + inner_width].T.astype(jnp.float32),
        gains_own[1],
        gains_own[2],
        gains_own[3],
        ffn_shard[:, :ff_width].astype(jnp.float32),
        ffn_shard[:, ff_step : ff_step + ff_width].astype(jnp.float32),
        ffn_shard[:, 2 * ff_step : 2 * ff_step + ff_width].astype(jnp.float32).T,
    )


def solution(mesh):
    placed = (
        P(("dp", "tensor"), None),
        P(("dp", "tensor"), None),
        P("dp"),
        P(("dp", "tensor")),
        P("dp"),
        P("dp", None),
        P("dp", None),
        P("dp", None),
        P(None, "dp"),
        P("dp", None, "tensor"),
        P(None, "dp"),
        P("dp"),
        P("dp", None),
        P(None, "dp"),
        P("dp"),
        P("dp"),
        P("dp"),
        P("tensor", "dp"),
        P("dp"),
        P("dp"),
        P("dp"),
        P("dp", "tensor"),
        P("dp", "tensor"),
        P("tensor", "dp"),
    )
    return jax.shard_map(
        per_device,
        mesh=mesh,
        in_specs=placed,
        out_specs=(
            P(("dp", "tensor"), None),
            P(("dp", "tensor"), None),
            P("dp"),
            P("dp", None),
            P("dp", None),
            P("dp", None),
            P(None, "dp"),
            P("dp", None, "tensor"),
            P(None, "dp"),
            P("dp"),
            P("dp", None),
            P(None, "dp"),
            P("dp"),
            P("dp"),
            P("dp"),
            P("tensor", "dp"),
            P("dp"),
            P("dp"),
            P("dp"),
            P("dp", "tensor"),
            P("dp", "tensor"),
            P("tensor", "dp"),
        ),
        check_vma=False,
    )
```

time: 4680 us -> 1290 us (0.28)
  waiting for transfers between devices: 1620 us -> 84.4 us
  other arithmetic: 1180 us -> 67 us
  matrix products: 1080 us -> 252 us
  Pallas kernels: 0 us -> 767 us
  local copies, waits for them, and re-layouts: 399 us -> 89.6 us
  blocking collectives: 261 us -> 0 us
  loops' own time: 104 us -> 0 us
    unnamed x34 -> x8, waiting for transfers between devices: 827 us -> 0.13 us
    pallas_call x0 -> x22, Pallas kernels: none -> 767 us  [the longest x5 200 us: reduce_rows(): pl.pallas_call(reduce_kernel, name='reduce_rows', in_specs=[whole], out_s...]
    dot_general x479 -> x1, matrix products: 738 us -> 10.1 us  [per_device(): lax.dot_general(out_w, grad_attn_whole, (((0,), (0,)), ((), ())), preferr...]
    reduce_scatter x7 -> x2, waiting for transfers between devices: 430 us -> 28.7 us  [per_device(): lax.psum_scatter(part, 'dp', scatter_dimension=0, tiled=True)]
    reduce_sum x77 -> x11, other arithmetic: 407 us -> 18.3 us  [the longest x3 8.6 us: normalize_t(): values * lax.rsqrt(jnp.mean(values * values, axis=0, keepdims=True) + EPS...]
    dot_general x64 -> x0, other arithmetic: 356 us -> none  [stretch_step(): jnp.einsum('tsc,ts,sc->tc', transfer, gram_matrix, drive_term, precision=...]
    all_gather x12 -> x5, waiting for transfers between devices: 360 us -> 55.5 us  [per_device(): gather_dp = lambda part: lax.all_gather(part, 'dp', axis=0, tiled=True)]
    convert_element_type x121 -> x15, other arithmetic: 234 us -> 33.5 us  [the longest x8 28.5 us: per_device(): low = lambda values: values.astype(jnp.bfloat16)]
  transfers between devices with their start and end apart: 27 -> 8, of which waited for: 17 -> 3; matrix products, arithmetic and copies ran while one was open for 54% -> 24% of each run, Pallas kernels for 0% -> 49%
where the time goes in v1:
time: 1290 us; the launch traced here: 1280 us
  Pallas kernels  767 us (59%)
  matrix products  252 us (20%)
  local copies, waits for them, and re-layouts  89.6 us (7%)
  waiting for transfers between devices  84.4 us (7%)
  other arithmetic  67 us (5%)
  between operations  17.9 us (1%)
    pallas_call x5, Pallas kernels, reduce_rows(): pl.pallas_call(reduce_kernel, name='reduce_rows', in_specs=[whole], out_s...  200 us
    pallas_call x5, Pallas kernels, gather_rows(): pl.pallas_call(gather_kernel, name='gather_rows', in_specs=[pl.BlockSpec(...  200 us
    dot_general x7, matrix products, dot_last(): lax.dot_general(left, right, (((1,), (1,)), ((), ())), preferred_element_...  113 us
    dot_general x8, matrix products, dot_first(): lax.dot_general(left, right, (((0,), (0,)), ((), ())), preferred_element_...  111 us
    pallas_call x3, Pallas kernels, weight_grads(): pl.pallas_call(functools.partial(weights_kernel, plan), name=name, grid=(...  87.5 us
    pallas_call x1, Pallas kernels, scan_backward(): pl.pallas_call(scan_bwd_kernel, name='scan_bwd', grid=(blocks,), in_specs...  69 us
    pallas_call x2, Pallas kernels, total_rows(): pl.pallas_call(total_kernel, name='total_rows', in_specs=[whole], out_spe...  58.4 us
    all_gather x5, waiting for transfers between devices, per_device(): gather_dp = lambda part: lax.all_gather(part, 'dp', axis=0, tiled=True)  55.5 us
  transfers between devices with their start and end apart: 8, of which 3 were waited for; matrix products, arithmetic and copies ran while one was open for 24% of the time, Pallas kernels for 49%

profile of v1, /device:TPU:17, one launch (start us, length us, event | category | flops | bytes accessed | tf_op | source)
XLA Modules:
  0.0 1278.2 jit_solution(15826816194736636911)
XLA Ops:
  16.3 11.2 hello.1
  28.7 2.4 fusion.17
  34.8 40.0 %gather_rows.5.refs_4_.refs_0_.refs_2_ = bf16[1600,2048]{1,0:T(8,128)(2,1)S(1)} custom-call(bf16[1600,512]{1,0:T(8,128)(2,1)S(1)} %multiply_convert_fusion.5.part_ref), custom_call_target="tpu_custom_call" | custom-call | bytes 147456000 | tf_op jit(solution)/shard_map/gather_rows/pallas_call | solution.py:129
  74.8 2.7 copy-done
  79.9 11.8 convolution_convert_fusion.3
  91.7 2.0 concatenate.72
  100.7 1.9 slice.255.qt_ref
  102.7 2.9 fusion.50
  109.5 31.5 %attn_fwd.1 = (bf16[640,2048]{1,0:T(8,128)(2,1)S(1)}, f32[2,8,2048]{2,1,0:T(8,128)S(1)}) custom-call(s32[16]{0:T(128)S(1)} %pad_add_fusion.4.first_ref, bf16[640,2048]{1,0:T(8,128)(2,1)S(1)} %slice.255.qt_ref, bf16[2,2048,64]{2,1,0:T(8,128)(2,1)S(1)} %bitcast.166, bf16[128,2048]{1,0:T(8,128)(2,1)S(1)} %copy-done.31, f32[1,2048]{1,0:T(1,128)S(1)} %bitcast.174, ...), custom_call_target="tpu_custom_call" | custom-call | bytes 207618048 | tf_op jit(solution)/shard_map/attn_fwd/pallas_call | solution.py:577
  143.5 34.2 %all-gather.8.cloned.1.call-done = bf16[1600,2144]{1,0:T(8,128)(2,1)} async-done(((bf16[200,2144]{1,0:T(8,128)(2,1)}), bf16[1600,2144]{1,0:T(8,128)(2,1)}) %all-gather.8.cloned.1.call-update) | async-done | bytes 6860816 | tf_op jit(solution)/shard_map/all_gather | solution.py:1161
  179.2 1.9 reshape.272
  185.1 10.8 fusion.27
  196.0 8.2 fusion.11
  206.0 18.0 %total_rows.2.dbl_ref = bf16[2048,256]{1,0:T(8,128)(2,1)S(1)} custom-call(f32[2048,256]{1,0:T(8,128)S(1)} %fusion.37.part_ref), custom_call_target="tpu_custom_call" | custom-call | bytes 62914560 | tf_op jit(solution)/shard_map/total_rows/pallas_call | solution.py:257
  225.2 13.4 %fusion.23.z_ref = f32[2048,800]{1,0:T(8,128)} fusion(bf16[1600,2048]{1,0:T(8,128)(2,1)} %copy-done, bf16[1600,2144]{1,0:T(8,128)(2,1)} %all-gather.8.cloned.1.call-done), kind=kOutput, calls=%fused_computation.74 | convolution fusion | flops 5242880000 | bytes 15974400 | tf_op jit(solution)/shard_map/dot_general | solution.py:46
  238.6 25.9 %scan_fwd.1 = (bf16[2048,800]{1,0:T(8,128)(2,1)S(1)}, f32[32,16,800]{2,1,0:T(8,128)S(1)}) custom-call(bf16[2048,800]{1,0:T(8,128)(2,1)S(1)} %copy-done.9, f32[2048,800]{1,0:T(8,128)} %fusion.23.z_ref, bf16[2048,256]{1,0:T(8,128)(2,1)S(1)} %copy-done.19, f32[2048,8]{1,0:T(8,128)S(1)} %copy-done.21, f32[1,2048]{1,0:T(1,128)S(1)} %bitcast.175, ...), custom_call_target="tpu_custom_call" | custom-call | bytes 97517568 | tf_op jit(solution)/shard_map/scan_fwd/pallas_call | solution.py:1047
  267.6 7.0 convolution_convert_fusion.2.part_ref
  274.6 39.7 %reduce_rows.5 = f32[1600,512]{1,0:T(8,128)S(1)} custom-call(bf16[1600,2048]{1,0:T(8,128)(2,1)S(1)} %convolution_convert_fusion.2.part_ref), custom_call_target="tpu_custom_call" | custom-call | bytes 147456000 | tf_op jit(solution)/shard_map/reduce_rows/pallas_call | solution.py:189
  314.4 7.5 convolution_convert_fusion.part_ref
  321.8 40.3 %reduce_rows.6 = f32[1600,512]{1,0:T(8,128)S(1)} custom-call(bf16[1600,2048]{1,0:T(8,128)(2,1)S(1)} %convolution_convert_fusion.part_ref), custom_call_target="tpu_custom_call" | custom-call | bytes 147456000 | tf_op jit(solution)/shard_map/reduce_rows/pallas_call | solution.py:189
  363.9 2.4 multiply_reduce_fusion.12
  371.5 39.9 %gather_rows.6.refs_0_.refs_2_ = bf16[1600,2048]{1,0:T(8,128)(2,1)S(1)} custom-call(bf16[1600,512]{1,0:T(8,128)(2,1)S(1)} %multiply_convert_fusion.4.part_ref), custom_call_target="tpu_custom_call" | custom-call | bytes 147456000 | tf_op jit(solution)/shard_map/gather_rows/pallas_call | solution.py:129
  411.4 2.8 copy-done.6
  414.2 17.7 %fusion.8 = f32[2048,1376]{1,0:T(8,128)} fusion(bf16[1600,2048]{1,0:T(8,128)(2,1)} %copy-done.6, bf16[1600,2816]{1,0:T(8,128)(2,1)} %all-gather.14.cloned.1.call-done), kind=kOutput, calls=%fused_computation.37 | convolution fusion | flops 9017753600 | bytes 22331392 | tf_op jit(solution)/shard_map/dot_general | solution.py:46
  431.9 19.0 %multiply_convert_fusion.2 = (bf16[2048,1376]{1,0:T(8,128)(2,1)}, f32[2048,1376]{1,0:T(8,128)}) fusion(f32[2048,1376]{1,0:T(8,128)} %fusion.8, bf16[1600,2048]{1,0:T(8,128)(2,1)S(1)} %copy-done.7, bf16[1600,2816]{1,0:T(8,128)(2,1)} %all-gather.14.cloned.1.call-done), kind=kOutput, calls=%fused_computation.4 | convolution fusion | flops 9034661888 | bytes 39501824 | tf_op jit(solution)/shard_map/dot_general | solution.py:46
  450.9 21.3 %all-gather.12.cloned.1.call-done = bf16[1600,1376]{1,0:T(8,128)(2,1)} async-done(((bf16[200,1376]{1,0:T(8,128)(2,1)}), bf16[1600,1376]{1,0:T(8,128)(2,1)}) %all-gather.12.cloned.1.call-update) | async-done | bytes 4403216 | tf_op jit(solution)/shard_map/all_gather | solution.py:1161
  472.2 14.1 %convolution_convert_fusion.1.part_ref = bf16[1600,2048]{1,0:T(8,128)(2,1)S(1)} fusion(bf16[1600,1376]{1,0:T(8,128)(2,1)} %all-gather.12.cloned.1.call-done, bf16[2048,1376]{1,0:T(8,128)(2,1)} %get-tuple-element.361.refs_5_), kind=kOutput, calls=%fused_computation.8 | convolution fusion | flops 9021030400 | bytes 16592896 | tf_op jit(solution)/shard_map/dot_general | solution.py:40
  486.4 40.7 %reduce_rows.7 = f32[1600,512]{1,0:T(8,128)S(1)} custom-call(bf16[1600,2048]{1,0:T(8,128)(2,1)S(1)} %convolution_convert_fusion.1.part_ref), custom_call_target="tpu_custom_call" | custom-call | bytes 147456000 | tf_op jit(solution)/shard_map/reduce_rows/pallas_call | solution.py:189
  528.5 39.9 %gather_rows.7.refs_4_ = bf16[1600,2048]{1,0:T(8,128)(2,1)S(1)} custom-call(bf16[1600,512]{1,0:T(8,128)(2,1)S(1)} %fusion.34.part_ref), custom_call_target="tpu_custom_call" | custom-call | bytes 147456000 | tf_op jit(solution)/shard_map/gather_rows/pallas_call | solution.py:129
  568.5 2.7 copy-done.13
  571.2 26.5 %multiply_convert_fusion = (bf16[2048,1376]{1,0:T(8,128)(2,1)}, bf16[2048,1376]{1,0:T(8,128)(2,1)}) fusion(f32[2048,1376]{1,0:T(8,128)} %fusion.8, f32[2048,1376]{1,0:T(8,128)} %get-tuple-element.362, bf16[1600,2048]{1,0:T(8,128)(2,1)} %copy-done.13, bf16[1600,1376]{1,0:T(8,128)(2,1)} %all-gather.12.cloned.1.call-done), kind=kOutput, calls=%fused_computation.2 | convolution fusion | flops 9054388224 | bytes 44773376 | tf_op jit(solution)/shard_map/dot_general | solution.py:46
  597.6 40.9 %ffn_weight_grads.1 = bf16[1600,4224]{1,0:T(8,128)(2,1)} custom-call(bf16[1600,2048]{1,0:T(8,128)(2,1)} %copy-done.6, bf16[2048,1376]{1,0:T(8,128)(2,1)} %get-tuple-element.112.refs_1_, bf16[1600,2048]{1,0:T(8,128)(2,1)} %copy-done.6, bf16[2048,1376]{1,0:T(8,128)(2,1)} %get-tuple-element.113.refs_3_, bf16[1600,2048]{1,0:T(8,128)(2,1)} %copy-done.13, ...), custom_call_target="tpu_custom_call" | custom-call | bytes 165675008 | tf_op jit(solution)/shard_map/ffn_weight_grads/pallas_call | solution.py:386
  638.6 16.7 %fusion.6 = f32[1600,2048]{1,0:T(8,128)} fusion(bf16[2048,1376]{1,0:T(8,128)(2,1)} %get-tuple-element.112.refs_1_, bf16[1600,2816]{1,0:T(8,128)(2,1)} %all-gather.14.cloned.1.call-done), kind=kOutput, calls=%fused_computation.35 | convolution fusion | flops 9017753600 | bytes 23379968 | tf_op jit(solution)/shard_map/dot_general | solution.py:40
  655.4 17.8 %add_convert_fusion.1.part_ref = bf16[1600,2048]{1,0:T(8,128)(2,1)} fusion(f32[1600,2048]{1,0:T(8,128)} %fusion.6, bf16[2048,1376]{1,0:T(8,128)(2,1)} %get-tuple-element.113.refs_3_, bf16[1600,2816]{1,0:T(8,128)(2,1)} %all-gather.14.cloned.1.call-done), kind=kOutput, calls=%fused_computation.1 | convolution fusion | flops 9024307200 | bytes 29933568 | tf_op jit(solution)/shard_map/dot_general | solution.py:40
  673.2 2.9 copy-done.28
  676.0 39.7 %reduce_rows.8 = f32[1600,512]{1,0:T(8,128)S(1)} custom-call(bf16[1600,2048]{1,0:T(8,128)(2,1)S(1)} %copy-done.28), custom_call_target="tpu_custom_call" | custom-call | bytes 147456000 | tf_op jit(solution)/shard_map/reduce_rows/pallas_call | solution.py:189
  718.8 6.3 multiply_reduce_fusion.8
  726.8 39.9 %gather_rows.8.refs_2_ = bf16[1600,2048]{1,0:T(8,128)(2,1)S(1)} custom-call(bf16[1600,512]{1,0:T(8,128)(2,1)S(1)} %get-tuple-element.334.part_ref), custom_call_target="tpu_custom_call" | custom-call | bytes 147456000 | tf_op jit(solution)/shard_map/gather_rows/pallas_call | solution.py:129
  766.7 40.0 %gather_rows.9.refs_0_ = bf16[1600,2048]{1,0:T(8,128)(2,1)S(1)} custom-call(bf16[1600,512]{1,0:T(8,128)(2,1)S(1)} %get-tuple-element.115.part_ref), custom_call_target="tpu_custom_call" | custom-call | bytes 147456000 | tf_op jit(solution)/shard_map/gather_rows/pallas_call | solution.py:129
  806.7 2.7 copy-done.11
  809.4 10.1 fusion.19.gs_ref
  819.5 69.0 %scan_bwd.1 = (bf16[2048,800]{1,0:T(8,128)(2,1)}, f32[2048,800]{1,0:T(8,128)}, f32[2048,256]{1,0:T(8,128)}, f32[100,800]{1,0:T(8,128)S(1)}, f32[8,800]{1,0:T(8,128)S(1)}) custom-call(bf16[2048,800]{1,0:T(8,128)(2,1)} %copy-done.8, f32[2048,800]{1,0:T(8,128)} %fusion.23.z_ref, bf16[2048,256]{1,0:T(8,128)(2,1)S(1)} %copy-done.20, f32[2048,8]{1,0:T(8,128)S(1)} %copy-done.22, ...), custom_call_target="tpu_custom_call" | custom-call | bytes 255852544 | tf_op jit(solution)/shard_map/scan_bwd/pallas_call | solution.py:1074
  888.5 26.6 %mid_weight_grads.1 = bf16[1600,2560]{1,0:T(8,128)(2,1)} custom-call(bf16[1600,2048]{1,0:T(8,128)(2,1)} %copy-done.11, bf16[640,2048]{1,0:T(8,128)(2,1)} %copy-done.16, bf16[1600,2048]{1,0:T(8,128)(2,1)} %copy-done.12, bf16[2048,800]{1,0:T(8,128)(2,1)} %copy-done.33, bf16[1600,2048]{1,0:T(8,128)(2,1)} %copy-done, bf16[2048,800]{1,0:T(8,128)(2,1)} %get-tuple-element.120.refs_5_), custom_call_target="tpu_custom_call" | custom-call | bytes 97517568 | tf_op jit(solution)/shard_map/mid_weight_grads/pallas_call | solution.py:386
  916.7 10.1 convolution_convert_fusion.4.dot_ref
  926.8 37.0 %attn_bwd.1 = (bf16[640,2048]{1,0:T(8,128)(2,1)S(1)}, f32[2,2048,64]{2,1,0:T(8,128)S(1)}, f32[2,2048,64]{2,1,0:T(8,128)S(1)}) custom-call(s32[16]{0:T(128)S(1)} %copy-done.48, bf16[640,2048]{1,0:T(8,128)(2,1)S(1)} %copy-done.15, bf16[640,2048]{1,0:T(8,128)(2,1)} %convolution_convert_fusion.4.dot_ref, bf16[640,2048]{1,0:T(8,128)(2,1)} %copy-done.16, ...), custom_call_target="tpu_custom_call" | custom-call | bytes 199229440 | tf_op jit(solution)/shard_map/attn_bwd/pallas_call | solution.py:668
  969.5 2.7 convert_bitcast_fusion.2
  972.2 2.3 copy.222
  975.1 3.2 pad_maximum_fusion.refs_3_
  978.3 40.4 %total_rows.3 = bf16[2048,256]{1,0:T(8,128)(2,1)S(1)} custom-call(f32[2048,256]{1,0:T(8,128)S(1)} %copy-done.37), custom_call_target="tpu_custom_call" | custom-call | bytes 62914560 | tf_op jit(solution)/shard_map/total_rows/pallas_call | solution.py:257
  1020.3 27.6 %multiply_reduce_fusion.2 = (f32[800]{0:T(1024)S(1)}, f32[800]{0:T(1024)S(1)}, f32[800]{0:T(1024)S(1)}, f32[800]{0:T(1024)S(1)}, bf16[800]{0:T(1024)(128)(2,1)S(...) fusion(f32[1,2048,800]{2,1,0:T(8,128)} %bitcast.180, ...), kind=kOutput, calls=%fused_computation.21 | convolution fusion | flops 883093760 | bytes 53741376 | tf_op jit(solution)/shard_map/dot_general | solution.py:40
  1050.6 12.8 %fusion.10.refs_1_ = bf16[2048,800]{1,0:T(8,128)(2,1)} fusion(f32[1,2048,800]{2,1,0:T(8,128)} %get-tuple-element.307, f32[1,2048,800]{2,1,0:T(8,128)} %get-tuple-element.308, f32[1,2048,800]{2,1,0:T(8,128)} %get-tuple-element.309, f32[1,2048,800]{2,1,0:T(8,128)} %get-tuple-element.310), kind=kLoop, calls=%fused_computation.39 | loop fusion | flops 6553600 | bytes 29491200 | tf_op jit(solution)/shard_map/convert_element_type | solution.py:1160
  1063.4 20.0 %last_weight_grads.1 = bf16[1600,2304]{1,0:T(8,128)(2,1)} custom-call(bf16[1600,2048]{1,0:T(8,128)(2,1)} %copy-done, bf16[2048,800]{1,0:T(8,128)(2,1)} %fusion.10.refs_1_, bf16[1600,2048]{1,0:T(8,128)(2,1)} %copy-done, bf16[896,2048]{1,0:T(8,128)(2,1)} %pad_maximum_fusion.refs_3_, bf16[1600,480]{1,0:T(8,128)(2,1)S(1)} %reshape.278.refs_4_), custom_call_target="tpu_custom_call" | custom-call | bytes 75497472 | tf_op jit(solution)/shard_map/last_weight_grads/pallas_call | solution.py:386
  1084.8 1.8 convert_bitcast_fusion.1
  1086.7 11.9 fusion.25
  1098.6 9.4 fusion.55
  1108.0 17.5 %add_convert_fusion.part_ref = bf16[1600,2048]{1,0:T(8,128)(2,1)} fusion(f32[1600,2048]{1,0:T(8,128)} %fusion.55, f32[1600,2048]{1,0:T(8,128)} %fusion.25, bf16[2048,800]{1,0:T(8,128)(2,1)} %get-tuple-element.120.refs_5_, bf16[1600,2144]{1,0:T(8,128)(2,1)} %all-gather.8.cloned.1.call-done), kind=kOutput, calls=%fused_computation | convolution fusion | flops 5252710400 | bytes 39305216 | tf_op jit(solution)/shard_map/dot_general | solution.py:40
  1125.6 2.9 copy-done.27
  1128.5 39.7 %reduce_rows.9 = f32[1600,512]{1,0:T(8,128)S(1)} custom-call(bf16[1600,2048]{1,0:T(8,128)(2,1)S(1)} %copy-done.27), custom_call_target="tpu_custom_call" | custom-call | bytes 147456000 | tf_op jit(solution)/shard_map/reduce_rows/pallas_call | solution.py:189
  1169.3 24.0 %farewell.1 = f32[8,256]{1,0:T(8,128)S(1)} custom-call(f32[8,8,256]{2,1,0:T(8,128)S(1)} %pad.44.part_ref), custom_call_target="tpu_custom_call" | custom-call | bytes 41943040 | tf_op jit(solution)/shard_map/farewell/pallas_call | solution.py:452
  1193.4 2.1 convert_bitcast_fusion.4
  1195.5 6.1 fusion.15
  1201.6 28.7 %reduce-scatter.8.cloned.1.call-done = bf16[200,2304]{1,0:T(8,128)(2,1)} async-done(((bf16[1600,2304]{1,0:T(8,128)(2,1)}), bf16[200,2304]{1,0:T(8,128)(2,1)}) %reduce-scatter.8.cloned.1.call-update) | async-done | bytes 921616 | tf_op jit(solution)/shard_map/reduce_scatter | solution.py:1162
  1233.4 22.5 %gather_stack.1 = bf16[4,200,2048]{2,1,0:T(8,128)(2,1)S(1)} custom-call(bf16[200,2048]{1,0:T(8,128)(2,1)S(1)} %fusion.36.part_ref), custom_call_target="tpu_custom_call" | custom-call | bytes 62914560 | tf_op jit(solution)/shard_map/gather_stack/pallas_call | solution.py:501
  1260.3 1.8 copy.227
  (434 shorter events, 83.0 us)
Async XLA Ops:
  7.2 72.7 %all-gather.6.cloned.1.call-start = ((), (), s32[]{:S(2)}) async-start(), calls=%async_computation.3 | async-start | bytes 3225600 | tf_op jit(solution)/shard_map/all_gather | solution.py:1161
  10.5 167.3 %all-gather.8.cloned.1.call-start = ((), (), s32[]{:S(2)}) async-start(), calls=%async_computation.4 | async-start | bytes 7833600 | tf_op jit(solution)/shard_map/all_gather | solution.py:1161
  34.8 44.1 %copy-start.66 = (bf16[800,200]{0,1:T(8,128)(2,1)S(1)}, bf16[800,200]{0,1:T(8,128)(2,1)}, u32[]{:S(2)}) copy-start(bf16[800,200]{0,1:T(8,128)(2,1)} %param.41) | copy-start | bytes 960004
  34.8 232.7 %all-gather.10.cloned.1.call-start = ((), (), s32[]{:S(2)}) async-start(), calls=%async_computation.5 | async-start | bytes 5529600 | tf_op jit(solution)/shard_map/all_gather | solution.py:1161
  79.8 11.9 copy-start.63
  79.8 11.9 copy-start.64
  79.8 14.5 %copy-start.65 = (s32[2048]{0:T(1024)S(1)}, s32[2048]{0:T(1024)}, u32[]{:S(2)}) copy-start(s32[2048]{0:T(1024)} %param.26) | copy-start | bytes 24580
  79.8 334.4 %all-gather.14.cloned.1.call-start = ((), (), s32[]{:S(2)}) async-start(), calls=%async_computation.7 | async-start | bytes 10137600 | tf_op jit(solution)/shard_map/all_gather | solution.py:1161
  93.7 378.5 %all-gather.12.cloned.1.call-start = ((), (), s32[]{:S(2)}) async-start(), calls=%async_computation.6 | async-start | bytes 5068800 | tf_op jit(solution)/shard_map/all_gather | solution.py:1161
  94.3 144.2 %copy-start.43 = (f32[2048]{0:T(1024)}, f32[2048]{0:T(1024)S(1)}, u32[]{:S(2)}) copy-start(f32[2048]{0:T(1024)S(1)} %convert_element_type.132) | copy-start | bytes 24580
  94.5 109.7 %copy-start.128 = (bf16[256]{0:T(256)(128)(2,1)}, bf16[256]{0:T(256)(128)(2,1)S(1)}, u32[]{:S(2)}) copy-start(bf16[256]{0:T(256)(128)(2,1)S(1)} %pad.72.clone) | copy-start | bytes 1540
  94.6 109.7 %copy-start.130 = (bf16[256]{0:T(256)(128)(2,1)}, bf16[256]{0:T(256)(128)(2,1)S(1)}, u32[]{:S(2)}) copy-start(bf16[256]{0:T(256)(128)(2,1)S(1)} %pad.74.clone) | copy-start | bytes 1540
  97.6 271.8 %copy-start.78 = (f32[1600]{0:T(1024)}, f32[1600]{0:T(1024)S(1)}, u32[]{:S(2)}) copy-start(f32[1600]{0:T(1024)S(1)} %mul.506) | copy-start | bytes 19204
  100.7 95.2 %copy-start.87 = (f32[1,2048]{1,0:T(1,128)}, f32[1,2048]{1,0:T(1,128)S(1)}, u32[]{:S(2)}) copy-start(f32[1,2048]{1,0:T(1,128)S(1)} %get-tuple-element.354) | copy-start | bytes 24580
  100.7 95.2 %copy-start.89 = (f32[1,2048]{1,0:T(1,128)}, f32[1,2048]{1,0:T(1,128)S(1)}, u32[]{:S(2)}) copy-start(f32[1,2048]{1,0:T(1,128)S(1)} %get-tuple-element.355) | copy-start | bytes 24580
  100.7 95.2 %copy-start.91 = (f32[1,2048]{1,0:T(1,128)}, f32[1,2048]{1,0:T(1,128)S(1)}, u32[]{:S(2)}) copy-start(f32[1,2048]{1,0:T(1,128)S(1)} %get-tuple-element.356) | copy-start | bytes 24580
  102.7 38.4 %copy-start.14 = (bf16[640,2048]{1,0:T(8,128)(2,1)}, bf16[640,2048]{1,0:T(8,128)(2,1)S(1)}, u32[]{:S(2)}) copy-start(bf16[640,2048]{1,0:T(8,128)(2,1)S(1)} %slice.255.qt_ref) | copy-start | bytes 7864324
  105.5 35.5 %copy-start.29 = (bf16[128,2048]{1,0:T(8,128)(2,1)}, bf16[128,2048]{1,0:T(8,128)(2,1)S(1)}, u32[]{:S(2)}) copy-start(bf16[128,2048]{1,0:T(8,128)(2,1)S(1)} %get-tuple-element.313.kt_ref) | copy-start | bytes 1572868
  183.5 20.7 %copy-start.75 = (bf16[800,100]{0,1:T(8,128)(2,1)}, bf16[800,100]{0,1:T(8,128)(2,1)S(1)}, u32[]{:S(2)}) copy-start(bf16[800,100]{0,1:T(8,128)(2,1)S(1)} %copy.240) | copy-start | bytes 480004
  184.9 19.3 %copy-start.83 = (bf16[800,32]{0,1:T(8,128)(2,1)}, bf16[800,32]{0,1:T(8,128)(2,1)S(1)}, u32[]{:S(2)}) copy-start(bf16[800,32]{0,1:T(8,128)(2,1)S(1)} %copy.241) | copy-start | bytes 153604
  184.9 53.6 %copy-start.45 = (f32[8,800]{1,0:T(8,128)}, f32[8,800]{1,0:T(8,128)S(1)}, u32[]{:S(2)}) copy-start(f32[8,800]{1,0:T(8,128)S(1)} %convert_bitcast_fusion.5.vec_ref) | copy-start | bytes 76804
  185.0 10.9 copy-start.112
  185.0 10.9 copy-start.114
  185.0 10.9 copy-start.116
  185.0 10.9 copy-start.118
  225.2 13.4 %copy-start.41 = (bf16[800,100]{0,1:T(8,128)(2,1)}, bf16[800,100]{0,1:T(8,128)(2,1)S(1)}, u32[]{:S(2)}) copy-start(bf16[800,100]{0,1:T(8,128)(2,1)S(1)} %copy.242) | copy-start | bytes 480004
  225.2 13.4 %copy-start.9 = (bf16[2048,800]{1,0:T(8,128)(2,1)S(1)}, bf16[2048,800]{1,0:T(8,128)(2,1)}, u32[]{:S(2)}) copy-start(bf16[2048,800]{1,0:T(8,128)(2,1)} %copy-done.8) | copy-start | bytes 9830404
  225.2 13.4 %copy-start.19 = (bf16[2048,256]{1,0:T(8,128)(2,1)S(1)}, bf16[2048,256]{1,0:T(8,128)(2,1)}, u32[]{:S(2)}) copy-start(bf16[2048,256]{1,0:T(8,128)(2,1)} %copy-done.18) | copy-start | bytes 3145732
  225.2 13.4 %copy-start.21 = (f32[2048,8]{1,0:T(8,128)S(1)}, f32[2048,8]{1,0:T(8,128)}, u32[]{:S(2)}) copy-start(f32[2048,8]{1,0:T(8,128)} %copy.203.mask_ref) | copy-start | bytes 196612
  238.6 28.9 %copy-start.17 = (bf16[640,2048]{1,0:T(8,128)(2,1)S(1)}, bf16[640,2048]{1,0:T(8,128)(2,1)}, u32[]{:S(2)}) copy-start(bf16[640,2048]{1,0:T(8,128)(2,1)} %copy-done.16) | copy-start | bytes 7864324
  274.6 39.7 %copy-start.34 = (bf16[2048,800]{1,0:T(8,128)(2,1)S(1)}, bf16[2048,800]{1,0:T(8,128)(2,1)}, u32[]{:S(2)}) copy-start(bf16[2048,800]{1,0:T(8,128)(2,1)} %copy-done.33) | copy-start | bytes 9830404
  274.6 39.7 %copy-start.126 = (bf16[1600,1440]{1,0:T(8,128)(2,1)S(1)}, bf16[1600,1440]{1,0:T(8,128)(2,1)}, u32[]{:S(2)}) copy-start(bf16[1600,1440]{1,0:T(8,128)(2,1)} %all-gather.10.cloned.1.call-done) | copy-start | bytes 13824004
  314.3 53.1 %copy-start.1 = (f32[1600,512]{1,0:T(8,128)}, f32[1600,512]{1,0:T(8,128)S(1)}, u32[]{:S(2)}) copy-start(f32[1600,512]{1,0:T(8,128)S(1)} %reduce_rows.5) | copy-start | bytes 9830404
  363.8 551.3 %reduce-scatter.10.cloned.1.call-start = ((), (), s32[]{:S(2)}) async-start(), calls=%async_computation.10 | async-start | bytes 15206400
  414.2 17.7 %copy-start.7 = (bf16[1600,2048]{1,0:T(8,128)(2,1)S(1)}, bf16[1600,2048]{1,0:T(8,128)(2,1)}, u32[]{:S(2)}) copy-start(bf16[1600,2048]{1,0:T(8,128)(2,1)} %copy-done.6) | copy-start | bytes 19660804
  486.3 40.8 %copy-start.50 = (f32[1600,512]{1,0:T(8,128)S(1)}, f32[1600,512]{1,0:T(8,128)}, u32[]{:S(2)}) copy-start(f32[1600,512]{1,0:T(8,128)} %copy-done.49) | copy-start | bytes 9830404
  486.3 40.8 %copy-start.59 = (f32[512,1600]{0,1:T(8,128)S(1)}, f32[512,1600]{0,1:T(8,128)}, u32[]{:S(2)}) copy-start(f32[512,1600]{0,1:T(8,128)} %param.25) | copy-start | bytes 9830404
  486.3 40.8 %copy-start.103 = (f32[512]{0:T(512)S(1)}, f32[512]{0:T(512)}, u32[]{:S(2)}) copy-start(f32[512]{0:T(512)} %convert_multiply_fusion) | copy-start | bytes 6148
  638.6 444.9 %reduce-scatter.6.cloned.1.call-start = ((), (), s32[]{:S(2)}) async-start(), calls=%async_computation.8 | async-start | bytes 9216000 | tf_op jit(solution)/shard_map/reduce_scatter | solution.py:1162
  676.0 39.8 %copy-start.51 = (f32[1600,512]{1,0:T(8,128)S(1)}, f32[1600,512]{1,0:T(8,128)}, u32[]{:S(2)}) copy-start(f32[1600,512]{1,0:T(8,128)} %copy-done.49) | copy-start | bytes 9830404
  676.0 39.8 %copy-start.79 = (f32[1600]{0:T(1024)S(1)}, f32[1600]{0:T(1024)}, u32[]{:S(2)}) copy-start(f32[1600]{0:T(1024)} %copy-done.78) | copy-start | bytes 19204
  676.0 39.8 %copy-start.94 = (f32[512]{0:T(512)S(1)}, f32[512]{0:T(512)}, u32[]{:S(2)}) copy-start(f32[512]{0:T(512)} %copy-done.93) | copy-start | bytes 6148
  726.8 82.6 %slice-start.2 = ((s8[4915200]{0:T(1024)(128)(4,1)}), s8[4194304]{0:T(1024)(128)(4,1)S(1)}, s32[]{:S(2)}) async-start(s8[4915200]{0:T(1024)(128)(4,1)} %bitcast.202), calls=%async_computation.13 | async-start | bytes 8388608
  766.6 40.0 %copy-start.12 = (bf16[1600,2048]{1,0:T(8,128)(2,1)}, bf16[1600,2048]{1,0:T(8,128)(2,1)S(1)}, u32[]{:S(2)}) copy-start(bf16[1600,2048]{1,0:T(8,128)(2,1)S(1)} %gather_rows.8.refs_2_) | copy-start | bytes 19660804
  766.6 42.7 %slice-start.3 = ((s8[4915200]{0:T(1024)(128)(4,1)}), s8[720896]{0:T(1024)(128)(4,1)S(1)}, s32[]{:S(2)}) async-start(s8[4915200]{0:T(1024)(128)(4,1)} %bitcast.202), calls=%async_computation.14 | async-start | bytes 1441792
  809.3 10.1 copy-start.20
  809.3 10.1 copy-start.22
  809.3 10.1 copy-start.40
  809.3 10.1 copy-start.42
  809.4 10.1 copy-start.44
  809.4 10.1 copy-start.46
  915.2 315.1 %reduce-scatter.8.cloned.1.call-start = ((), (), s32[]{:S(2)}) async-start(), calls=%async_computation.9 | async-start | bytes 8294400 | tf_op jit(solution)/shard_map/reduce_scatter | solution.py:1162
  916.7 10.1 copy-start.15
  916.7 10.1 copy-start.24
  916.7 10.1 copy-start.26
  975.1 43.6 %copy-start.10 = (bf16[2048,800]{1,0:T(8,128)(2,1)S(1)}, bf16[2048,800]{1,0:T(8,128)(2,1)}, u32[]{:S(2)}) copy-start(bf16[2048,800]{1,0:T(8,128)(2,1)} %copy-done.8) | copy-start | bytes 9830404
  1020.3 27.7 %copy-start.102 = (bf16[800,3]{0,1:T(4,128)(2,1)S(1)}, bf16[800,3]{0,1:T(4,128)(2,1)}, u32[]{:S(2)}) copy-start(bf16[800,3]{0,1:T(4,128)(2,1)} %slice_bitcast_fusion.25) | copy-start | bytes 14404
  1086.7 11.9 copy-start.57
  1086.7 11.9 copy-start.127
  1128.5 39.8 %copy-start.54 = (f32[512,1600]{0,1:T(8,128)S(1)}, f32[512,1600]{0,1:T(8,128)}, u32[]{:S(2)}) copy-start(f32[512,1600]{0,1:T(8,128)} %param.24) | copy-start | bytes 9830404
  1128.5 39.8 %copy-start.81 = (f32[1600]{0:T(1024)S(1)}, f32[1600]{0:T(1024)}, u32[]{:S(2)}) copy-start(f32[1600]{0:T(1024)} %copy-done.80) | copy-start | bytes 19204
  1128.5 39.8 %copy-start.97 = (f32[512]{0:T(512)S(1)}, f32[512]{0:T(512)}, u32[]{:S(2)}) copy-start(f32[512]{0:T(512)} %copy-done.96) | copy-start | bytes 6148
  1168.3 25.1 %copy-start.107 = (f32[512]{0:T(512)S(1)}, f32[512]{0:T(512)}, u32[]{:S(2)}) copy-start(f32[512]{0:T(512)} %copy-done.106) | copy-start | bytes 6148
  1195.5 37.7 %slice-start.1 = ((bf16[200,2560]{1,0:T(8,128)(2,1)}), bf16[200,640]{1,0:T(8,128)(2,1)S(1)}, s32[]{:S(2)}) async-start(bf16[200,2560]{1,0:T(8,128)(2,1)} %reduce-scatter.6.cloned.1.call-done), calls=%async_computation.12 | async-start | bytes 512000 | tf_op jit(solution)/shard_map/slice | solution.py:1395
  (80 other events, 233.5 us)
Sparse Core Ops, SparseCore 0:
  10.8 58.3 all-gather.5
  72.0 105.7 all-gather.7
  180.5 80.4 all-gather.9
  263.6 131.0 all-gather.13
  396.7 75.4 all-gather.11
  638.7 218.8 reduce-scatter.9
  915.3 144.2 reduce-scatter.5
  1083.6 146.6 reduce-scatter.7
